TPU v7x, 32 devices: a whole 2x2x4 slice. The times are simulated.
32 devices in a mesh: lon: 2 (over y), lat: 4 (over z), depth: 4 (over x, core).
Axes of the slice: x: 2, y: 2, z: 4, core: 2. Of those that a mesh axis runs over, the one named last changes fastest.
Arguments:
- snapshots: float32 [32768, 256], P(('lon', 'lat', 'depth')), may hold values from -300 to 300
- live_rows: int32 [32], P(('lon', 'lat', 'depth')), may hold values from 128 to 1024, as said below
- column_order: int32 [256], replicated, may hold values from 0 to 255, each once
Outputs:
- snapshot_basis: float32 [32768, 256], P(('lon', 'lat', 'depth'))
- triangular: float32 [256, 256], replicated
- highpass: float32 [32768, 256], P(('lon', 'lat', 'depth'))
Inputs may be any that keep to these rules, and one draw needn't show every extreme that they name: `live_rows`: each entry is a multiple of 128; some block has all 1024 rows live and some other block has 128.
All inputs are finite; a program needn't handle non-finite values.
Results may differ from a plain program's by a relative error of at most 0.00005.
Values sent between devices are 32-bit elements; how exact they have to be, the bound alone decides.
No kernel may reach another device: no remote copies, remote signals or barrier semaphores. Data moves between devices by JAX's collectives and lax.ppermute only.
A program may use at most 64 MiB of HBM per device.

v0:
```python
import jax
import jax.numpy as jnp
from jax import lax
from jax.sharding import PartitionSpec as P

LOW = 32


def on_device(snapshots, live_rows, column_order):
    row_count = snapshots.shape[0]
    total_rows = row_count * lax.axis_size("lon") * lax.axis_size("lat") * lax.axis_size("depth")
    picked = jnp.take(snapshots, column_order, axis=1)
    live_mask = (lax.iota(jnp.int32, row_count) < live_rows[0])[:, None]
    masked = jnp.where(live_mask, picked, jnp.zeros_like(picked))
    local_gram = (
        lax.dot_general(masked, masked, (((0,), (0,)), ((), ())), precision=lax.Precision.HIGHEST)
        / total_rows
    )
    global_gram = lax.psum(local_gram, ("lon", "lat", "depth"))
    lower_factor = jnp.linalg.cholesky(global_gram)
    triangular = lower_factor.T
    snapshot_basis = jax.scipy.linalg.solve_triangular(lower_factor, masked.T, lower=True).T
    highpass = masked - jnp.dot(
        snapshot_basis[:, :LOW], triangular[:LOW, :], precision=lax.Precision.HIGHEST
    )
    return (snapshot_basis, triangular, highpass)


def solution(mesh):
    placed = (P(("lon", "lat", "depth"), None), P(("lon", "lat", "depth")), P())
    return jax.shard_map(
        on_device,
        mesh=mesh,
        in_specs=placed,
        out_specs=(P(("lon", "lat", "depth"), None), P(), P(("lon", "lat", "depth"), None)),
        check_vma=False,
    )
```

profile of v0, /device:TPU:0, one launch (start us, length us, event | category | flops | bytes accessed | tf_op | source)
XLA Modules:
  0.0 216.7 jit_solution(15282165486884055820)
XLA Ops:
  7.2 0.0 all-reduce.3.cloned.1.call-start
  7.2 0.7 compare_select_fusion
  7.9 0.0 copy-done.1
  7.9 1.6 copy.6
  9.5 1.1 gather_fusion
  10.6 0.3 copy.7
  11.6 0.2 select_select_fusion
  11.8 2.5 %convolution_multiply_fusion = f32[256,256]{0,1:T(8,128)} fusion(f32[256,1024]{0,1:T(8,128)S(1)} %select_select_fusion), kind=kOutput, calls=%fused_computation.5 | convolution fusion | flops 805371904 | bytes 1310720 | tf_op jit(solution)/shard_map/dot_general | solution.py:16
  14.3 0.0 all-reduce.3.cloned.1.call-update
  14.4 127.8 %all-reduce.3.cloned.1.call-done = f32[256,256]{0,1:T(8,128)} async-done(((f32[256,256]{0,1:T(8,128)}), f32[256,256]{0,1:T(8,128)}) %all-reduce.3.cloned.1.call-update) | async-done | bytes 262160 | tf_op jit(solution)/shard_map/psum | solution.py:19
  142.2 1.1 copy.9
  143.4 11.7 %cholesky.50 = f32[128,128]{1,0:T(8,128)S(1)} custom-call(f32[128,128]{1,0:T(8,128)S(1)} %cholesky.118), custom_call_target="Cholesky" | custom-call | tf_op jit(solution)/shard_map/jit(cholesky)/cholesky | solution.py:20
  155.1 9.8 %custom-call.15 = f32[1,128,128]{1,2,0:T(8,128)S(1)} custom-call(f32[1,128,128]{2,1,0:T(8,128)S(1)} %get-tuple-element.29), custom_call_target="InvertDiagBlocksLowerTriangular" | custom-call | tf_op jit(solution)/shard_map/jit(cholesky)/cholesky | solution.py:20
  165.0 0.3 fusion.9
  165.3 0.1 copy.10
  165.3 0.3 convolution_subtract_fusion.2
  165.7 11.9 %cholesky.105 = f32[128,128]{1,0:T(8,128)S(1)} custom-call(f32[128,128]{1,0:T(8,128)S(1)} %convolution_subtract_fusion.2), custom_call_target="Cholesky" | custom-call | tf_op jit(solution)/shard_map/jit(cholesky)/cholesky | solution.py:20
  177.6 0.6 compare_reduce_fusion
  179.6 0.1 triangular_solve.60
  179.6 4.0 %while.1 = (s32[]{:T(128)}, f32[256,256]{1,0:T(8,128)S(1)}, s32[2,2]{1,0:T(2,128)S(1)}, f32[2,128,128]{2,1,0:T(8,128)S(1)}, s32[]{:T(128)}) while((s32[]{:T(128)}, f32[256,256]{1,0:T(8,128)S(1)}, s32[2,2]{1,0:T(2,128)S(1)}, f32[2,128,128]{2,1,0:T(8,128)S(1)}, s32[]{:T(128)}) %tuple.28), condition=%wide.while_cond, body=%wide.while_body.sunk | while | flops 2 | bytes 131181 | solution.py:22
  179.6 0.6 fusion.20
  180.2 1.4 bitcast_dynamic-update-slice_fusion.2
  181.7 0.6 fusion.20
  182.2 1.4 bitcast_dynamic-update-slice_fusion.2
  183.6 19.7 %custom-call.16 = f32[2,128,128]{1,2,0:T(8,128)S(1)} custom-call(f32[2,128,128]{2,1,0:T(8,128)S(1)} %get-tuple-element.10), custom_call_target="InvertDiagBlocksLowerTriangular" | custom-call | tf_op jit(solution)/shard_map/jit(_solve_triangular)/triangular_solve | solution.py:22
  203.3 0.6 fusion
  204.0 1.0 convolution_subtract_fusion.1
  205.0 0.6 fusion.8
  205.6 0.1 maximum_bitcast_fusion
  205.7 1.3 copy.11
  207.0 2.0 convolution_subtract_fusion
  209.0 0.8 copy.12
  (17 shorter events, 0.2 us)
Async XLA Ops:
  7.2 0.8 copy-start.1
  7.2 135.0 %all-reduce.3.cloned.1.call-start = ((), (), s32[]{:S(2)}) async-start(), calls=%async_computation | async-start | bytes 524288 | tf_op jit(solution)/shard_map/psum | solution.py:19
  142.2 1.2 copy-start
Sparse Core Ops, SparseCore 0:
  14.5 127.6 all-reduce.2
where the time goes:
time: 217 us
  waiting for transfers between devices  128 us (59%)
  other arithmetic  54.9 us (25%)
  between operations  16.2 us (7%)
  local copies, waits for them, and re-layouts  10.4 us (5%)
  matrix products  7.37 us (3%)
    psum x1, waiting for transfers between devices, on_device(): global_gram = lax.psum(local_gram, ('lon', 'lat', 'depth'))  128 us
    another operation x6, other arithmetic, on_device(): lower_factor = jnp.linalg.cholesky(global_gram)  34.1 us
    another operation x2, other arithmetic, on_device(): jax.scipy.linalg.solve_triangular(lower_factor, masked.T, lower=True)  19.7 us
  transfers between devices with their start and end apart: 1, of which 1 were waited for; matrix products, arithmetic and copies ran while one was open for 0% of the time, Pallas kernels for 0%

commit v1 on v0

v1 whole, which is shorter than its diff:
```python
import functools

import jax
import jax.numpy as jnp
from jax import lax
from jax.experimental import pallas as pl
from jax.experimental.pallas import tpu as pltpu
from jax.sharding import PartitionSpec as P

LOW = 32
HALF = 128
TILE = 8
AXES = ("lon", "lat", "depth")
HIGHEST = lax.Precision.HIGHEST
VMEM_LIMIT = 48 * 1024 * 1024


def dot(a, b, dims=((1,), (0,))):
    return lax.dot_general(
        a, b, (dims, ((), ())), precision=HIGHEST, preferred_element_type=jnp.float32
    )


def one_hot(order_ref):
    count = order_ref.shape[1]
    source = lax.broadcasted_iota(jnp.int32, (count, count), 0)
    return jnp.where(source == order_ref[...], 1.0, 0.0).astype(jnp.float32)


def gram_kernel(live_ref, order_ref, x_ref, gram_ref, *, total_rows):
    rows = lax.broadcasted_iota(jnp.int32, x_ref.shape, 0)
    masked = jnp.where(rows < live_ref[0], x_ref[...], 0.0)
    gram = dot(masked, masked, ((0,), (0,))) / total_rows
    pick = one_hot(order_ref)
    gram_ref[...] = dot(pick, dot(gram, pick), ((0,), (0,)))


def sum_kernel(parts_ref, out_ref):
    total = jnp.sum(parts_ref[...], axis=0)
    out_ref[...] = jnp.broadcast_to(total[None], out_ref.shape)


def spread(value):
    return jnp.broadcast_to(value, (TILE, HALF))


def factor(matrix, upper_ref, inverse_ref, beside):
    steps = HALF // TILE
    lanes = lax.broadcasted_iota(jnp.int32, (TILE, HALF), 1)
    subs = lax.broadcasted_iota(jnp.int32, (TILE, HALF), 0)
    trail = [matrix[g * TILE : (g + 1) * TILE] for g in range(steps)]
    eye = [jnp.where(lanes == subs + g * TILE, 1.0, 0.0) for g in range(steps)]
    for s in range(steps):
        first = s * TILE
        column = [
            [spread(trail[g][:, first + m : first + m + 1]) for m in range(TILE)]
            for g in range(s, steps)
        ]
        d = [[spread(column[0][q][i : i + 1]) for q in range(i + 1)] for i in range(TILE)]
        r = [spread(trail[s][m : m + 1]) for m in range(TILE)]
        t = [spread(eye[s][m : m + 1]) for m in range(TILE)]
        ahead = list(column[1]) if s + 1 < steps else None
        inv = [None] * TILE
        for m in range(TILE):
            inv[m] = lax.rsqrt(d[m][m])
            for i in range(m + 1, TILE):
                d[i][m] = d[i][m] * inv[m]
            for q in range(m + 1, TILE):
                for i in range(q, TILE):
                    d[i][q] = d[i][q] - d[i][m] * d[q][m]
            r[m] = r[m] * inv[m]
            t[m] = t[m] * inv[m]
            for i in range(m + 1, TILE):
                r[i] = r[i] - d[i][m] * r[m]
                t[i] = t[i] - d[i][m] * t[m]
            if ahead is not None:
                ahead[m] = ahead[m] * inv[m]
                for q in range(m + 1, TILE):
                    ahead[q] = ahead[q] - d[q][m] * ahead[m]
        for m in range(TILE):
            upper_ref[first + m : first + m + 1, :] = r[m][0:1]
            inverse_ref[first + m : first + m + 1, :] = t[m][0:1]
        if ahead is not None:
            for m in range(TILE):
                trail[s + 1] = trail[s + 1] - ahead[m] * r[m]
                eye[s + 1] = eye[s + 1] - ahead[m] * t[m]
        if s + 2 < steps:
            zr, zt = list(r), list(t)
            for m in reversed(range(TILE)):
                zr[m] = zr[m] * inv[m]
                zt[m] = zt[m] * inv[m]
                for i in range(m):
                    zr[i] = zr[i] - d[m][i] * zr[m]
                    zt[i] = zt[i] - d[m][i] * zt[m]
            for g in range(s + 2, steps):
                for m in range(TILE):
                    trail[g] = trail[g] - column[g - s][m] * zr[m]
                    eye[g] = eye[g] - column[g - s][m] * zt[m]
        beside(s)


def finish_kernel(
    live_ref, order_ref, gram_ref, x_ref,
    basis_ref, tri_ref, high_ref,
    upper, inverse, picked, rest,
):
    rows = x_ref.shape[0]
    steps = HALF // TILE
    chunk = rows // steps
    pick = one_hot(order_ref)

    def pick_rows(s):
        at = slice(s * chunk, (s + 1) * chunk)
        row = lax.broadcasted_iota(jnp.int32, (chunk, x_ref.shape[1]), 0) + s * chunk
        picked[at] = dot(jnp.where(row < live_ref[0], x_ref[at], 0.0), pick)

    above = lax.broadcasted_iota(jnp.int32, (HALF, HALF), 0) <= lax.broadcasted_iota(
        jnp.int32, (HALF, HALF), 1
    )
    factor(gram_ref[:HALF, :HALF], upper, inverse, pick_rows)
    tri_ref[:HALF, :HALF] = jnp.where(above, upper[...], 0.0)
    tri_ref[HALF:, :HALF] = jnp.zeros((HALF, HALF), jnp.float32)
    first_inverse = inverse[...]
    corner = dot(first_inverse, gram_ref[:HALF, HALF:])
    tri_ref[:HALF, HALF:] = corner
    second = gram_ref[HALF:, HALF:] - dot(corner, corner, ((0,), (0,)))

    def first_half(s):
        at = slice(s * chunk, (s + 1) * chunk)
        left = dot(picked[at, :HALF], first_inverse, ((1,), (1,)))
        basis_ref[at, :HALF] = left
        rest[at] = picked[at, HALF:] - dot(left, corner)
        high_ref[at] = picked[at] - dot(left[:, :LOW], tri_ref[:LOW, :])

    factor(second, upper, inverse, first_half)
    tri_ref[HALF:, HALF:] = jnp.where(above, upper[...], 0.0)
    basis_ref[:, HALF:] = dot(rest[...], inverse[...], ((1,), (1,)))


def sum_over_devices(gram, devices):
    width = gram.shape[0]
    if width % (TILE * devices):
        return lax.psum(gram, AXES)
    parts = lax.all_to_all(gram.reshape(devices, width // devices, width), AXES, 0, 0)
    total = pl.pallas_call(
        sum_kernel, out_shape=jax.ShapeDtypeStruct(parts.shape, jnp.float32)
    )(parts)
    return lax.all_to_all(total, AXES, 0, 0).reshape(width, width)


def on_device(snapshots, live_rows, column_order, *, devices):
    rows, width = snapshots.shape
    smem = pl.BlockSpec(memory_space=pltpu.SMEM)
    vmem = pl.BlockSpec(memory_space=pltpu.VMEM)
    params = pltpu.CompilerParams(vmem_limit_bytes=VMEM_LIMIT)
    order = column_order.reshape(1, width)
    square = jax.ShapeDtypeStruct((width, width), jnp.float32)
    tall = jax.ShapeDtypeStruct((rows, width), jnp.float32)
    gram = pl.pallas_call(
        functools.partial(gram_kernel, total_rows=rows * devices),
        in_specs=[smem, vmem, vmem],
        out_specs=vmem,
        out_shape=square,
        compiler_params=params,
    )(live_rows, order, snapshots)
    gram = sum_over_devices(gram, devices)
    return pl.pallas_call(
        finish_kernel,
        in_specs=[smem, vmem, vmem, vmem],
        out_specs=[vmem, vmem, vmem],
        out_shape=[tall, square, tall],
        scratch_shapes=[
            pltpu.VMEM((HALF, HALF), jnp.float32),
            pltpu.VMEM((HALF, HALF), jnp.float32),
            pltpu.VMEM((rows, width), jnp.float32),
            pltpu.VMEM((rows, HALF), jnp.float32),
        ],
        compiler_params=params,
    )(live_rows, order, gram, snapshots)


def solution(mesh):
    placed = (P(AXES, None), P(AXES), P())
    return jax.shard_map(
        functools.partial(on_device, devices=mesh.size),
        mesh=mesh,
        in_specs=placed,
        out_specs=(P(AXES, None), P(), P(AXES, None)),
        check_vma=False,
    )
```

time: 217 us -> 53.1 us (0.24)
  waiting for transfers between devices: 128 us -> 0 us
  other arithmetic: 54.9 us -> 0 us
  blocking collectives: 0 us -> 30.4 us
  Pallas kernels: 0 us -> 19.2 us
  between operations: 16.2 us -> 1.3 us
  local copies, waits for them, and re-layouts: 10.4 us -> 1.9 us
  matrix products: 7.37 us -> 0 us
    psum x1 -> x0, waiting for transfers between devices: 128 us -> none  [on_device(): global_gram = lax.psum(local_gram, ('lon', 'lat', 'depth'))]
    another operation x8 -> x0, other arithmetic: 53.8 us -> none  [the longest x6 34.1 us: on_device(): lower_factor = jnp.linalg.cholesky(global_gram)]
    all_to_all x0 -> x2, blocking collectives: none -> 30.4 us  [the longest x1 17.5 us: sum_over_devices(): lax.all_to_all(gram.reshape(devices, width // devices, width), AXES, 0, 0)]
    pallas_call x0 -> x3, Pallas kernels: none -> 19.2 us  [the longest x1 15.1 us: on_device(): pl.pallas_call(finish_kernel, in_specs=[smem, vmem, vmem, vmem], out_spec...]
    dot_general x2 -> x0, matrix products: 4.52 us -> none  [the longest x1 2.52 us: on_device(): lax.dot_general(masked, masked, (((0,), (0,)), ((), ())), precision=lax.P...]
    another operation x11 -> x0, local copies, waits for them, and re-layouts: 4.15 us -> none
    another operation x5 -> x0, matrix products: 2.85 us -> none  [the longest x3 2.27 us: on_device(): jax.scipy.linalg.solve_triangular(lower_factor, masked.T, lower=True)]
  transfers between devices with their start and end apart: 1 -> 0, of which waited for: 1 -> 0; matrix products, arithmetic and copies ran while one was open for 0% -> 0% of each run, Pallas kernels for 0% -> 0%
where the time goes in v1:
time: 53.1 us; the launch traced here: 52.8 us
  blocking collectives  30.4 us (57%)
  Pallas kernels  19.2 us (36%)
  local copies, waits for them, and re-layouts  1.9 us (4%)
  between operations  1.3 us (2%)
    all_to_all x1, blocking collectives, sum_over_devices(): lax.all_to_all(gram.reshape(devices, width // devices, width), AXES, 0, 0)  17.5 us
    pallas_call x1, Pallas kernels, on_device(): pl.pallas_call(finish_kernel, in_specs=[smem, vmem, vmem, vmem], out_spec...  15.1 us
    all_to_all x1, blocking collectives, sum_over_devices(): return lax.all_to_all(total, AXES, 0, 0).reshape(width, width)  12.9 us
    pallas_call x1, Pallas kernels, on_device(): pl.pallas_call(functools.partial(gram_kernel, total_rows=rows * devices),...  2.42 us
    unnamed x6, local copies, waits for them, and re-layouts  1.9 us
    pallas_call x1, Pallas kernels, sum_over_devices(): pl.pallas_call(sum_kernel, out_shape=jax.ShapeDtypeStruct(parts.shape, jn...  1.7 us

profile of v1, /device:TPU:0, one launch (start us, length us, event | category | flops | bytes accessed | tf_op | source)
XLA Modules:
  0.0 52.8 jit_solution(6489569463227015378)
XLA Ops:
  1.3 0.0 copy-start.2
  1.3 0.7 %copy-done.2 = s32[256]{0:T(256)S(1)} copy-done((s32[256]{0:T(256)S(1)}, s32[256]{0:T(256)}, u32[]{:S(2)}) %copy-start.2) | copy-done | bytes 1048
  2.0 0.0 copy-start
  2.0 1.2 %copy-done = f32[1024,256]{1,0:T(8,128)S(1)} copy-done((f32[1024,256]{1,0:T(8,128)S(1)}, f32[1024,256]{1,0:T(8,128)}, u32[]{:S(2)}) %copy-start) | copy-done | bytes 1048600
  3.2 2.4 %shard_map.58 = f32[256,256]{1,0:T(8,128)S(1)} custom-call(s32[1]{0:T(128)S(6)} %copy.6.live_ref, s32[1,256]{1,0:T(1,128)S(1)} %bitcast.5, f32[1024,256]{1,0:T(8,128)S(1)} %copy-done), custom_call_target="tpu_custom_call" | custom-call | tf_op jit(solution)/shard_map/pallas_call | solution.py:159
  5.6 0.0 copy-start.1
  5.6 17.5 %all_to_all.10.parts_ref = f32[32,8,256]{2,1,0:T(8,128)} all-to-all(f32[32,8,256]{2,1,0:T(8,128)S(1)} %bitcast.4), channel_id=1, replica_groups=mesh['lon'=2,'lat'=4,'depth'=4] {'lon','lat','depth'}, dimensions={0} | all-to-all | bytes 524288 | tf_op jit(solution)/shard_map/all_to_all | solution.py:144
  23.1 1.7 %shard_map.59 = f32[32,8,256]{2,1,0:T(8,128)} custom-call(f32[32,8,256]{2,1,0:T(8,128)} %all_to_all.10.parts_ref), custom_call_target="tpu_custom_call" | custom-call | tf_op jit(solution)/shard_map/pallas_call | solution.py:145
  24.8 12.9 %all_to_all.11 = f32[32,8,256]{2,1,0:T(8,128)S(1)} all-to-all(f32[32,8,256]{2,1,0:T(8,128)} %shard_map.59), channel_id=1, replica_groups=mesh['lon'=2,'lat'=4,'depth'=4] {'lon','lat','depth'}, dimensions={0} | all-to-all | bytes 524288 | tf_op jit(solution)/shard_map/all_to_all | solution.py:148
  37.7 0.0 copy-done.1
  37.7 15.1 %shard_map.60 = (f32[1024,256]{1,0:T(8,128)}, f32[256,256]{1,0:T(8,128)}, f32[1024,256]{1,0:T(8,128)}) custom-call(s32[1]{0:T(128)S(6)} %copy.6.live_ref, s32[1,256]{1,0:T(1,128)S(1)} %bitcast.6, f32[256,256]{1,0:T(8,128)S(1)} %bitcast.3, f32[1024,256]{1,0:T(8,128)S(1)} %copy-done.1), custom_call_target="tpu_custom_call" | custom-call | tf_op jit(solution)/shard_map/pallas_call | solution.py:167
Async XLA Ops:
  1.3 0.7 %copy-start.2 = (s32[256]{0:T(256)S(1)}, s32[256]{0:T(256)}, u32[]{:S(2)}) copy-start(s32[256]{0:T(256)} %param.5) | copy-start | bytes 3076
  2.0 1.2 %copy-start = (f32[1024,256]{1,0:T(8,128)S(1)}, f32[1024,256]{1,0:T(8,128)}, u32[]{:S(2)}) copy-start(f32[1024,256]{1,0:T(8,128)} %x_ref.3) | copy-start | bytes 3145732
  5.6 32.1 %copy-start.1 = (f32[1024,256]{1,0:T(8,128)S(1)}, f32[1024,256]{1,0:T(8,128)}, u32[]{:S(2)}) copy-start(f32[1024,256]{1,0:T(8,128)} %x_ref.3) | copy-start | bytes 3145732

commit v2 on v0

v2 whole, which is shorter than its diff:
```python
import functools

import jax
import jax.numpy as jnp
from jax import lax
from jax.experimental import pallas as pl
from jax.experimental.pallas import tpu as pltpu
from jax.sharding import PartitionSpec as P

LOW = 32
HALF = 128
TILE = 8
WIDE = 2
AXES = ("lon", "lat", "depth")
HIGHEST = lax.Precision.HIGHEST
VMEM_LIMIT = 16 * 1024 * 1024
LOADS = 4
PIECES = 8


def dot(a, b, dims=((1,), (0,)), precision=None):
    return lax.dot_general(
        a, b, (dims, ((), ())), precision=precision, preferred_element_type=jnp.float32
    )


def halves(value):
    high = value.astype(jnp.bfloat16)
    return high, (value - high.astype(jnp.float32)).astype(jnp.bfloat16)


def one_hot(order_ref):
    count = order_ref.shape[1]
    source = lax.broadcasted_iota(jnp.int32, (count, count), 0)
    return jnp.where(source == order_ref[...], 1.0, 0.0).astype(jnp.bfloat16)


def square_iotas():
    return (
        lax.broadcasted_iota(jnp.int32, (HALF, HALF), 0),
        lax.broadcasted_iota(jnp.int32, (HALF, HALF), 1),
    )


def gram_kernel(live_ref, order_ref, x_ref, packed_ref, picked_ref, held, sems, *, total_rows):
    rows, width = held.shape
    chunk = rows // LOADS
    copies = []
    for c in range(LOADS):
        at = pl.ds(c * chunk, chunk)
        copies.append(pltpu.make_async_copy(x_ref.at[at], held.at[at], sems.at[c]))
        copies[-1].start()
    pick = one_hot(order_ref)
    both = jnp.zeros((width, width), jnp.float32)
    cross = jnp.zeros((width, width), jnp.float32)
    for c in range(LOADS):
        at = slice(c * chunk, (c + 1) * chunk)
        copies[c].wait()
        row = lax.broadcasted_iota(jnp.int32, (chunk, width), 0) + c * chunk
        x = jnp.where(row < live_ref[0], held[at], 0.0)
        high = x.astype(jnp.bfloat16)
        left = x - high.astype(jnp.float32)
        middle = left.astype(jnp.bfloat16)
        low = (left - middle.astype(jnp.float32)).astype(jnp.bfloat16)
        high, middle, low = dot(high, pick), dot(middle, pick), dot(low, pick)
        picked_ref[at] = high + (middle + low)
        high = high.astype(jnp.bfloat16)
        middle = middle.astype(jnp.bfloat16)
        low = low.astype(jnp.bfloat16)
        down = ((0,), (0,))
        both = both + (dot(high, high, down) + dot(middle, middle, down))
        cross = cross + (dot(high, middle, down) + dot(high, low, down))
    gram = (both + (cross + cross.T)) / total_rows
    i, j = square_iotas()
    packed_ref[:HALF] = gram[:HALF, HALF:]
    last = gram[HALF:, HALF:]
    packed_ref[HALF : 2 * HALF] = jnp.where(i <= j, gram[:HALF, :HALF], last)
    packed_ref[2 * HALF :] = jnp.zeros((packed_ref.shape[0] - 2 * HALF, HALF), jnp.float32)
    packed_ref[2 * HALF : 2 * HALF + 1] = jnp.sum(jnp.where(i == j, last, 0.0), 0, keepdims=True)


def sum_kernel(parts_ref, out_ref, *, devices):
    each = parts_ref.shape[0] // devices
    terms = [parts_ref[k * each : (k + 1) * each] for k in range(devices)]
    while len(terms) > 1:
        pairs = [a + b for a, b in zip(terms[::2], terms[1::2])]
        terms = pairs + terms[len(pairs) * 2 :]
    for k in range(devices):
        out_ref[k * each : (k + 1) * each] = terms[0]


def spread(value):
    return jnp.broadcast_to(value, (TILE, HALF))


def factor(matrix, upper_ref, inverse_ref, update_ref, beside):
    width = WIDE * TILE
    steps = HALF // width
    groups = HALF // TILE
    lanes = lax.broadcasted_iota(jnp.int32, (TILE, HALF), 1)
    subs = lax.broadcasted_iota(jnp.int32, (TILE, HALF), 0)
    rows = [matrix[g * TILE : (g + 1) * TILE] for g in range(groups)]
    update_ref[...] = jnp.zeros_like(update_ref)
    for s in range(steps):
        first = s * width
        mine = range(s * WIDE, (s + 1) * WIDE)
        near = range((s + 1) * WIDE, min((s + 2) * WIDE, groups))
        far = range((s + 2) * WIDE, groups)
        column = [[spread(rows[g][:, first + q : first + q + 1]) for g in mine] for q in range(width)]
        side = {
            g: [spread(rows[g][:, first + q : first + q + 1]) for q in range(width)] for g in near
        }
        panel = [rows[g] for g in mine]
        up, low, scale = [None] * WIDE, [None] * WIDE, [None] * WIDE
        for m in range(width):
            home, at = divmod(m, TILE)
            here = subs == at
            pivot = spread(column[m][home][at : at + 1])
            recip = 1.0 / pivot
            root = lax.rsqrt(pivot)
            times = list(column[m])
            times[home] = jnp.where(here, 0.0, times[home])
            times = [value * recip for value in times]
            for q in range(m + 1, width):
                value = spread(column[q][home][at : at + 1])
                column[q] = [c - t * value for c, t in zip(column[q], times)]
            row_up = spread(panel[home][at : at + 1]) * root
            lane = lanes == first + m
            panel = [
                jnp.where(lane, jnp.where(here, 1.0, 0.0) if h == home else 0.0, panel[h])
                for h in range(WIDE)
            ]
            row = spread(panel[home][at : at + 1])
            row_low = row * root
            if at:
                up[home] = jnp.where(here, row_up, up[home])
                low[home] = jnp.where(here, row_low, low[home])
                scale[home] = jnp.where(here, recip, scale[home])
            else:
                up[home], low[home], scale[home] = row_up, row_low, recip
            panel = [p - t * row for p, t in zip(panel, times)]
        for h, g in enumerate(mine):
            at = slice(g * TILE, (g + 1) * TILE)
            upper_ref[at] = jnp.where(lanes >= subs + g * TILE, up[h], 0.0)
            inverse_ref[at] = jnp.where(lanes <= subs + g * TILE, low[h], 0.0)
        inside = (lanes >= first) & (lanes < first + width)
        solved = [p * c for p, c in zip(panel, scale)]
        for g in near:
            terms = [
                side[g][h * TILE + i] * spread(solved[h][i : i + 1])
                for h in range(WIDE)
                for i in range(TILE)
            ]
            while len(terms) > 1:
                terms = [a + b for a, b in zip(terms[::2], terms[1::2])]
            rows[g] = jnp.where(inside, 0.0, rows[g]) - terms[0]
        if far:
            for h, g in enumerate(mine):
                update_ref[g * TILE : (g + 1) * TILE] = solved[h]
            if s:
                update_ref[first - width : first] = jnp.zeros((width, HALF), jnp.float32)
            change = dot(
                jnp.concatenate([rows[g] for g in far], 0), update_ref[...], precision=HIGHEST
            )
            for k, g in enumerate(far):
                rows[g] = jnp.where(inside, 0.0, rows[g]) - change[k * TILE : (k + 1) * TILE]
        beside(s)


def finish_kernel(
    packed_ref, picked_ref, basis_ref, tri_ref, high_ref,
    basis, tri, high, rest, upper, inverse, update, sems,
):
    rows = picked_ref.shape[0]
    chunk = rows // PIECES
    i, j = square_iotas()
    mixed = packed_ref[HALF : 2 * HALF]
    flipped = mixed.T
    first = jnp.where(i <= j, mixed, flipped)
    last = jnp.where(i > j, mixed, flipped)
    last = jnp.where(
        i == j, jnp.broadcast_to(packed_ref[2 * HALF : 2 * HALF + 1], (HALF, HALF)), last
    )
    side = packed_ref[:HALF]

    copies = []

    def send(source, target, at, lanes):
        copies.append(
            pltpu.make_async_copy(
                source.at[at, lanes], target.at[at, lanes], sems.at[len(copies)]
            )
        )
        copies[-1].start()

    left_lanes, right_lanes, all_lanes = pl.ds(0, HALF), pl.ds(HALF, HALF), pl.ds(0, 2 * HALF)
    factor(first, upper, inverse, update, lambda s: None)
    corner = dot(inverse[...], side, precision=HIGHEST)
    tri[:HALF, :HALF] = upper[...]
    tri[:HALF, HALF:] = corner
    tri[HALF:, :HALF] = jnp.zeros((HALF, HALF), jnp.float32)
    second = last - dot(corner, corner, ((0,), (0,)), HIGHEST)

    none = jnp.zeros((HALF, HALF), jnp.bfloat16)

    def inverse_weights():
        h, l = halves(inverse[...])
        return jnp.concatenate([jnp.concatenate([h, h], 1), jnp.concatenate([l, none], 1)], 0)

    def fold(value):
        return value[:, :HALF] + value[:, HALF:]

    to_left = inverse_weights()
    ch, cl = halves(corner)
    to_rest = jnp.concatenate([jnp.concatenate([ch, cl], 1), jnp.concatenate([ch, none], 1)], 0)
    th, tl = halves(tri[:LOW, :])
    blank = jnp.zeros((HALF - LOW, 2 * HALF), jnp.bfloat16)
    to_high = jnp.concatenate([th, blank, th, blank], 0)
    to_high_low = jnp.concatenate([tl, blank], 0)

    def first_half(s):
        at = slice(s * chunk, (s + 1) * chunk)
        xh, xl = halves(picked_ref[at, :HALF])
        left = fold(dot(jnp.concatenate([xh, xl], 1), to_left, ((1,), (1,))))
        basis[at, :HALF] = left
        lh, ll = halves(left)
        both = jnp.concatenate([lh, ll], 1)
        rest[at] = picked_ref[at, HALF:] - fold(dot(both, to_rest))
        high[at] = picked_ref[at] - (dot(both, to_high) + dot(lh, to_high_low))
        rows_at = pl.ds(s * chunk, chunk)
        send(basis, basis_ref, rows_at, left_lanes)
        send(high, high_ref, rows_at, all_lanes)

    factor(second, upper, inverse, update, first_half)
    tri[HALF:, HALF:] = upper[...]
    send(tri, tri_ref, pl.ds(0, 2 * HALF), all_lanes)
    to_right = inverse_weights()
    for s in range(PIECES):
        at = slice(s * chunk, (s + 1) * chunk)
        rh, rl = halves(rest[at])
        basis[at, HALF:] = fold(dot(jnp.concatenate([rh, rl], 1), to_right, ((1,), (1,))))
        send(basis, basis_ref, pl.ds(s * chunk, chunk), right_lanes)
    for copy in copies:
        copy.wait()


def sum_over_devices(packed, devices):
    if packed.shape[0] % devices:
        return lax.psum(packed, AXES)
    shape = packed.shape

    def exchange(value):
        value = value.reshape(shape[0], 1, shape[1])
        return lax.all_to_all(value, AXES, 0, 0, tiled=True).reshape(shape)

    total = pl.pallas_call(
        functools.partial(sum_kernel, devices=devices),
        in_specs=[pl.BlockSpec(memory_space=pltpu.VMEM)],
        out_specs=pl.BlockSpec(memory_space=pltpu.VMEM),
        out_shape=jax.ShapeDtypeStruct(shape, jnp.float32),
        compiler_params=pltpu.CompilerParams(vmem_limit_bytes=VMEM_LIMIT),
    )(exchange(packed))
    return exchange(total)


def on_device(snapshots, live_rows, column_order, *, devices):
    rows, width = snapshots.shape
    smem = pl.BlockSpec(memory_space=pltpu.SMEM)
    vmem = pl.BlockSpec(memory_space=pltpu.VMEM)
    hbm = pl.BlockSpec(memory_space=pl.ANY)
    params = pltpu.CompilerParams(vmem_limit_bytes=VMEM_LIMIT)
    square = jax.ShapeDtypeStruct((width, width), jnp.float32)
    tall = jax.ShapeDtypeStruct((rows, width), jnp.float32)
    packed_rows = width + 32
    packed, picked = pl.pallas_call(
        functools.partial(gram_kernel, total_rows=rows * devices),
        in_specs=[smem, vmem, hbm],
        out_specs=[vmem, vmem],
        out_shape=[jax.ShapeDtypeStruct((packed_rows, HALF), jnp.float32), tall],
        scratch_shapes=[
            pltpu.VMEM((rows, width), jnp.float32),
            pltpu.SemaphoreType.DMA((LOADS,)),
        ],
        compiler_params=params,
    )(live_rows, column_order.reshape(1, width), snapshots)
    packed = sum_over_devices(packed, devices)
    block = pltpu.VMEM((HALF, HALF), jnp.float32)
    return pl.pallas_call(
        finish_kernel,
        in_specs=[vmem, vmem],
        out_specs=[hbm, hbm, hbm],
        out_shape=[tall, square, tall],
        scratch_shapes=[
            pltpu.VMEM((rows, width), jnp.float32),
            pltpu.VMEM((width, width), jnp.float32),
            pltpu.VMEM((rows, width), jnp.float32),
            pltpu.VMEM((rows, HALF), jnp.float32),
            block,
            block,
            block,
            pltpu.SemaphoreType.DMA((3 * PIECES + 1,)),
        ],
        compiler_params=params,
    )(packed, picked)


def solution(mesh):
    placed = (P(AXES, None), P(AXES), P())
    return jax.shard_map(
        functools.partial(on_device, devices=mesh.size),
        mesh=mesh,
        in_specs=placed,
        out_specs=(P(AXES, None), P(), P(AXES, None)),
        check_vma=False,
    )
```

time: 217 us -> 38.9 us (0.18)
  waiting for transfers between devices: 128 us -> 0 us
  other arithmetic: 54.9 us -> 0 us
  blocking collectives: 0 us -> 25.8 us
  between operations: 16.2 us -> 1.3 us
  Pallas kernels: 0 us -> 9.71 us
  local copies, waits for them, and re-layouts: 10.4 us -> 1.9 us
  matrix products: 7.37 us -> 0 us
    psum x1 -> x0, waiting for transfers between devices: 128 us -> none  [on_device(): global_gram = lax.psum(local_gram, ('lon', 'lat', 'depth'))]
    another operation x8 -> x0, other arithmetic: 53.8 us -> none  [the longest x6 34.1 us: on_device(): lower_factor = jnp.linalg.cholesky(global_gram)]
    all_to_all x0 -> x2, blocking collectives: none -> 25.8 us  [exchange(): return lax.all_to_all(value, AXES, 0, 0, tiled=True).reshape(shape)]
    pallas_call x0 -> x3, Pallas kernels: none -> 9.71 us  [the longest x1 7.27 us: on_device(): pl.pallas_call(finish_kernel, in_specs=[vmem, vmem], out_specs=[hbm, hbm,...]
    dot_general x2 -> x0, matrix products: 4.52 us -> none  [the longest x1 2.52 us: on_device(): lax.dot_general(masked, masked, (((0,), (0,)), ((), ())), precision=lax.P...]
    another operation x11 -> x0, local copies, waits for them, and re-layouts: 4.15 us -> none
    another operation x5 -> x0, matrix products: 2.85 us -> none  [the longest x3 2.27 us: on_device(): jax.scipy.linalg.solve_triangular(lower_factor, masked.T, lower=True)]
  transfers between devices with their start and end apart: 1 -> 0, of which waited for: 1 -> 0; matrix products, arithmetic and copies ran while one was open for 0% -> 0% of each run, Pallas kernels for 0% -> 0%
where the time goes in v2:
time: 38.9 us; the launch traced here: 38.7 us
  blocking collectives  25.8 us (66%)
  Pallas kernels  9.71 us (25%)
  local copies, waits for them, and re-layouts  1.9 us (5%)
  between operations  1.3 us (3%)
    all_to_all x2, blocking collectives, exchange(): return lax.all_to_all(value, AXES, 0, 0, tiled=True).reshape(shape)  25.8 us
    pallas_call x1, Pallas kernels, on_device(): pl.pallas_call(finish_kernel, in_specs=[vmem, vmem], out_specs=[hbm, hbm,...  7.27 us
    pallas_call x1, Pallas kernels, on_device(): pl.pallas_call(functools.partial(gram_kernel, total_rows=rows * devices),...  2.41 us
    unnamed x4, local copies, waits for them, and re-layouts  1.9 us

profile of v2, /device:TPU:0, one launch (start us, length us, event | category | flops | bytes accessed | tf_op | source)
XLA Modules:
  0.0 38.7 jit_solution(3080057279780781088)
XLA Ops:
  1.3 0.0 copy-start.1
  1.3 0.7 %copy-done.1 = s32[256]{0:T(256)S(1)} copy-done((s32[256]{0:T(256)S(1)}, s32[256]{0:T(256)}, u32[]{:S(2)}) %copy-start.1) | copy-done | bytes 1048
  2.0 0.0 copy-start
  2.0 1.2 %copy-done = f32[1024,256]{1,0:T(8,128)S(1)} copy-done((f32[1024,256]{1,0:T(8,128)S(1)}, f32[1024,256]{1,0:T(8,128)}, u32[]{:S(2)}) %copy-start) | copy-done | bytes 1048600
  3.2 2.4 %shard_map.58 = (f32[288,128]{1,0:T(8,128)S(1)}, f32[1024,256]{1,0:T(8,128)S(1)}) custom-call(s32[1]{0:T(128)S(6)} %copy.8.live_ref, s32[1,256]{1,0:T(1,128)S(1)} %bitcast.13, f32[1024,256]{1,0:T(8,128)S(1)} %copy-done), custom_call_target="tpu_custom_call" | custom-call | tf_op jit(solution)/shard_map/pallas_call | solution.py:275
  5.6 15.5 %all_to_all.10 = f32[288,1,128]{2,1,0:T(1,128)S(1)} all-to-all(f32[288,1,128]{2,1,0:T(1,128)S(1)} %bitcast.12), channel_id=1, replica_groups=mesh['lon'=2,'lat'=4,'depth'=4] {'lon','lat','depth'}, dimensions={0} | all-to-all | bytes 294912 | tf_op jit(solution)/shard_map/all_to_all | solution.py:254
  21.1 10.3 %all_to_all.11 = f32[288,1,128]{2,1,0:T(1,128)S(1)} all-to-all(f32[288,1,128]{2,1,0:T(1,128)S(1)} %bitcast.11), channel_id=1, replica_groups=mesh['lon'=2,'lat'=4,'depth'=4] {'lon','lat','depth'}, dimensions={0} | all-to-all | bytes 294912 | tf_op jit(solution)/shard_map/all_to_all | solution.py:254
  31.4 7.3 %shard_map.60 = (f32[1024,256]{1,0:T(8,128)}, f32[256,256]{1,0:T(8,128)}, f32[1024,256]{1,0:T(8,128)}) custom-call(f32[288,128]{1,0:T(8,128)S(1)} %bitcast.9, f32[1024,256]{1,0:T(8,128)S(1)} %get-tuple-element.6.picked_ref), custom_call_target="tpu_custom_call" | custom-call | tf_op jit(solution)/shard_map/pallas_call | solution.py:288
  (1 shorter events, 0.0 us)
Async XLA Ops:
  1.3 0.7 %copy-start.1 = (s32[256]{0:T(256)S(1)}, s32[256]{0:T(256)}, u32[]{:S(2)}) copy-start(s32[256]{0:T(256)} %param.5) | copy-start | bytes 3076
  2.0 1.2 %copy-start = (f32[1024,256]{1,0:T(8,128)S(1)}, f32[1024,256]{1,0:T(8,128)}, u32[]{:S(2)}) copy-start(f32[1024,256]{1,0:T(8,128)} %x_ref.1) | copy-start | bytes 3145732

commit v3 on v2

--- a/solution.py
+++ b/solution.py
@@ -12,9 +12,8 @@
 TILE = 8
 WIDE = 2
 AXES = ("lon", "lat", "depth")
-HIGHEST = lax.Precision.HIGHEST
 VMEM_LIMIT = 16 * 1024 * 1024
-LOADS = 4
+LOADS = 2
 PIECES = 8
 
 
@@ -42,14 +41,19 @@
     )
 
 
-def gram_kernel(live_ref, order_ref, x_ref, packed_ref, picked_ref, held, sems, *, total_rows):
+def gram_kernel(
+    live_ref, order_in, x_ref, packed_ref, picked_ref, held, order_ref, sems, *, total_rows
+):
     rows, width = held.shape
     chunk = rows // LOADS
+    fetch_order = pltpu.make_async_copy(order_in, order_ref, sems.at[LOADS])
+    fetch_order.start()
     copies = []
     for c in range(LOADS):
         at = pl.ds(c * chunk, chunk)
         copies.append(pltpu.make_async_copy(x_ref.at[at], held.at[at], sems.at[c]))
         copies[-1].start()
+    fetch_order.wait()
     pick = one_hot(order_ref)
     both = jnp.zeros((width, width), jnp.float32)
     cross = jnp.zeros((width, width), jnp.float32)
@@ -58,11 +62,7 @@
         copies[c].wait()
         row = lax.broadcasted_iota(jnp.int32, (chunk, width), 0) + c * chunk
         x = jnp.where(row < live_ref[0], held[at], 0.0)
-        high = x.astype(jnp.bfloat16)
-        left = x - high.astype(jnp.float32)
-        middle = left.astype(jnp.bfloat16)
-        low = (left - middle.astype(jnp.float32)).astype(jnp.bfloat16)
-        high, middle, low = dot(high, pick), dot(middle, pick), dot(low, pick)
+        high, middle, low = (dot(part, pick) for part in thirds(x))
         picked_ref[at] = high + (middle + low)
         high = high.astype(jnp.bfloat16)
         middle = middle.astype(jnp.bfloat16)
@@ -93,6 +93,22 @@
     return jnp.broadcast_to(value, (TILE, HALF))
 
 
+def thirds(value):
+    high = value.astype(jnp.bfloat16)
+    rest = value - high.astype(jnp.float32)
+    middle = rest.astype(jnp.bfloat16)
+    return high, middle, (rest - middle.astype(jnp.float32)).astype(jnp.bfloat16)
+
+
+def full_dot(a, b):
+    ah, am, al = thirds(a)
+    bh, bm, bl = thirds(b)
+    pair = jnp.concatenate([bh, bm], 1)
+    first = dot(jnp.concatenate([ah, am], 1), jnp.concatenate([pair, pair], 0))
+    second = dot(jnp.concatenate([ah, al], 1), jnp.concatenate([bl, bh], 0))
+    return first[:, :HALF] + (first[:, HALF:] + second)
+
+
 def factor(matrix, upper_ref, inverse_ref, update_ref, beside):
     width = WIDE * TILE
     steps = HALF // width
@@ -106,10 +122,14 @@
         mine = range(s * WIDE, (s + 1) * WIDE)
         near = range((s + 1) * WIDE, min((s + 2) * WIDE, groups))
         far = range((s + 2) * WIDE, groups)
-        column = [[spread(rows[g][:, first + q : first + q + 1]) for g in mine] for q in range(width)]
-        side = {
-            g: [spread(rows[g][:, first + q : first + q + 1]) for q in range(width)] for g in near
-        }
+
+
+        def pulled(g, q):
+            only = jnp.where(lanes == first + q, rows[g], 0.0)
+            return spread(jnp.sum(only, axis=1, keepdims=True))
+
+        column = [[pulled(g, q) for g in mine] for q in range(width)]
+        side = {g: [pulled(g, q) for q in range(width)] for g in near}
         panel = [rows[g] for g in mine]
         up, low, scale = [None] * WIDE, [None] * WIDE, [None] * WIDE
         for m in range(width):
@@ -159,9 +179,7 @@
                 update_ref[g * TILE : (g + 1) * TILE] = solved[h]
             if s:
                 update_ref[first - width : first] = jnp.zeros((width, HALF), jnp.float32)
-            change = dot(
-                jnp.concatenate([rows[g] for g in far], 0), update_ref[...], precision=HIGHEST
-            )
+            change = full_dot(jnp.concatenate([rows[g] for g in far], 0), update_ref[...])
             for k, g in enumerate(far):
                 rows[g] = jnp.where(inside, 0.0, rows[g]) - change[k * TILE : (k + 1) * TILE]
         beside(s)
@@ -195,11 +213,11 @@
 
     left_lanes, right_lanes, all_lanes = pl.ds(0, HALF), pl.ds(HALF, HALF), pl.ds(0, 2 * HALF)
     factor(first, upper, inverse, update, lambda s: None)
-    corner = dot(inverse[...], side, precision=HIGHEST)
+    corner = full_dot(inverse[...], side)
     tri[:HALF, :HALF] = upper[...]
     tri[:HALF, HALF:] = corner
     tri[HALF:, :HALF] = jnp.zeros((HALF, HALF), jnp.float32)
-    second = last - dot(corner, corner, ((0,), (0,)), HIGHEST)
+    second = last - full_dot(corner.T, corner)
 
     none = jnp.zeros((HALF, HALF), jnp.bfloat16)
 
@@ -263,6 +281,10 @@
     return exchange(total)
 
 
+def in_hbm(array):
+    return pltpu.with_memory_space_constraint(array, pltpu.HBM)
+
+
 def on_device(snapshots, live_rows, column_order, *, devices):
     rows, width = snapshots.shape
     smem = pl.BlockSpec(memory_space=pltpu.SMEM)
@@ -274,15 +296,16 @@
     packed_rows = width + 32
     packed, picked = pl.pallas_call(
         functools.partial(gram_kernel, total_rows=rows * devices),
-        in_specs=[smem, vmem, hbm],
+        in_specs=[smem, hbm, hbm],
         out_specs=[vmem, vmem],
         out_shape=[jax.ShapeDtypeStruct((packed_rows, HALF), jnp.float32), tall],
         scratch_shapes=[
             pltpu.VMEM((rows, width), jnp.float32),
-            pltpu.SemaphoreType.DMA((LOADS,)),
+            pltpu.VMEM((1, width), jnp.int32),
+            pltpu.SemaphoreType.DMA((LOADS + 1,)),
         ],
         compiler_params=params,
-    )(live_rows, column_order.reshape(1, width), snapshots)
+    )(live_rows, in_hbm(column_order.reshape(1, width)), in_hbm(snapshots))
     packed = sum_over_devices(packed, devices)
     block = pltpu.VMEM((HALF, HALF), jnp.float32)
     return pl.pallas_call(

time: 38.9 us -> 36.5 us (0.938)
  local copies, waits for them, and re-layouts: 1.9 us -> 0 us
  Pallas kernels: 9.71 us -> 9.22 us
    unnamed x4 -> x0, local copies, waits for them, and re-layouts: 1.9 us -> none
    pallas_call x1, Pallas kernels: 7.27 us -> 6.58 us  [on_device(): pl.pallas_call(finish_kernel, in_specs=[vmem, vmem], out_specs=[hbm, hbm,...]
where the time goes in v3:
time: 36.5 us; the launch traced here: 36.3 us
  blocking collectives  25.8 us (71%)
  Pallas kernels  9.22 us (25%)
  between operations  1.29 us (4%)
    all_to_all x2, blocking collectives, exchange(): return lax.all_to_all(value, AXES, 0, 0, tiled=True).reshape(shape)  25.8 us
    pallas_call x1, Pallas kernels, on_device(): pl.pallas_call(finish_kernel, in_specs=[vmem, vmem], out_specs=[hbm, hbm,...  6.58 us
    pallas_call x1, Pallas kernels, on_device(): pl.pallas_call(functools.partial(gram_kernel, total_rows=rows * devices),...  2.61 us

profile of v3, /device:TPU:0, one launch (start us, length us, event | category | flops | bytes accessed | tf_op | source)
XLA Modules:
  0.0 36.3 jit_solution(9116583664813120545)
XLA Ops:
  1.3 2.6 %shard_map.58 = (f32[288,128]{1,0:T(8,128)S(1)}, f32[1024,256]{1,0:T(8,128)S(1)}) custom-call(s32[1]{0:T(128)S(6)} %copy.8.live_ref, s32[1,256]{1,0:T(1,128)} %bitcast.13, f32[1024,256]{1,0:T(8,128)} %x_ref.1), custom_call_target="tpu_custom_call" | custom-call | tf_op jit(solution)/shard_map/pallas_call | solution.py:297
  3.9 15.5 %all_to_all.10 = f32[288,1,128]{2,1,0:T(1,128)S(1)} all-to-all(f32[288,1,128]{2,1,0:T(1,128)S(1)} %bitcast.12), channel_id=1, replica_groups=mesh['lon'=2,'lat'=4,'depth'=4] {'lon','lat','depth'}, dimensions={0} | all-to-all | bytes 294912 | tf_op jit(solution)/shard_map/all_to_all | solution.py:272
  19.5 10.3 %all_to_all.11 = f32[288,1,128]{2,1,0:T(1,128)S(1)} all-to-all(f32[288,1,128]{2,1,0:T(1,128)S(1)} %bitcast.11), channel_id=1, replica_groups=mesh['lon'=2,'lat'=4,'depth'=4] {'lon','lat','depth'}, dimensions={0} | all-to-all | bytes 294912 | tf_op jit(solution)/shard_map/all_to_all | solution.py:272
  29.7 6.6 %shard_map.60 = (f32[1024,256]{1,0:T(8,128)}, f32[256,256]{1,0:T(8,128)}, f32[1024,256]{1,0:T(8,128)}) custom-call(f32[288,128]{1,0:T(8,128)S(1)} %bitcast.9, f32[1024,256]{1,0:T(8,128)S(1)} %get-tuple-element.6.picked_ref), custom_call_target="tpu_custom_call" | custom-call | tf_op jit(solution)/shard_map/pallas_call | solution.py:311
  (1 shorter events, 0.0 us)

commit v4 on v3

--- a/solution.py
+++ b/solution.py
@@ -1,4 +1,6 @@
 import functools
+import itertools
+import math
 
 import jax
 import jax.numpy as jnp
@@ -77,16 +79,6 @@
     packed_ref[HALF : 2 * HALF] = jnp.where(i <= j, gram[:HALF, :HALF], last)
     packed_ref[2 * HALF :] = jnp.zeros((packed_ref.shape[0] - 2 * HALF, HALF), jnp.float32)
     packed_ref[2 * HALF : 2 * HALF + 1] = jnp.sum(jnp.where(i == j, last, 0.0), 0, keepdims=True)
-
-
-def sum_kernel(parts_ref, out_ref, *, devices):
-    each = parts_ref.shape[0] // devices
-    terms = [parts_ref[k * each : (k + 1) * each] for k in range(devices)]
-    while len(terms) > 1:
-        pairs = [a + b for a, b in zip(terms[::2], terms[1::2])]
-        terms = pairs + terms[len(pairs) * 2 :]
-    for k in range(devices):
-        out_ref[k * each : (k + 1) * each] = terms[0]
 
 
 def spread(value):
@@ -262,30 +254,47 @@
         copy.wait()
 
 
-def sum_over_devices(packed, devices):
-    if packed.shape[0] % devices:
+def flipped(value, sizes, moves):
+    axes = tuple(axis for axis, _ in moves)
+    pairs = []
+    for source in itertools.product(*(range(sizes[axis]) for axis in axes)):
+        target = [place ^ bit for place, (_, bit) in zip(source, moves)]
+        index = [0, 0]
+        for axis, a, b in zip(axes, source, target):
+            index = [index[0] * sizes[axis] + a, index[1] * sizes[axis] + b]
+        pairs.append(tuple(index))
+    return lax.ppermute(value, axes, pairs)
+
+
+def sum_over_devices(packed, sizes):
+    bits = [(axis, 1 << k) for axis in AXES for k in range(sizes[axis].bit_length() - 1)]
+    if any(size & (size - 1) for size in sizes.values()) or len(bits) < 4:
         return lax.psum(packed, AXES)
-    shape = packed.shape
-
-    def exchange(value):
-        value = value.reshape(shape[0], 1, shape[1])
-        return lax.all_to_all(value, AXES, 0, 0, tiled=True).reshape(shape)
-
-    total = pl.pallas_call(
-        functools.partial(sum_kernel, devices=devices),
-        in_specs=[pl.BlockSpec(memory_space=pltpu.VMEM)],
-        out_specs=pl.BlockSpec(memory_space=pltpu.VMEM),
-        out_shape=jax.ShapeDtypeStruct(shape, jnp.float32),
-        compiler_params=pltpu.CompilerParams(vmem_limit_bytes=VMEM_LIMIT),
-    )(exchange(packed))
-    return exchange(total)
+    split = ("depth", 1)
+    together = [("lon", 1), ("depth", 2)]
+    bits = [bit for bit in bits if bit != split and bit not in together]
+    half = packed.shape[0] // 2
+    mine = lax.axis_index("depth") & 1
+    parts = packed.reshape(2, half, packed.shape[1])
+    total = lax.dynamic_index_in_dim(parts, mine, 0, False) + flipped(
+        lax.dynamic_index_in_dim(parts, 1 - mine, 0, False), sizes, [split]
+    )
+    first = flipped(total, sizes, together[:1])
+    second = flipped(total, sizes, together[1:])
+    third = flipped(total, sizes, together)
+    total = (total + first) + (second + third)
+    for bit in bits:
+        total = total + flipped(total, sizes, [bit])
+    other = flipped(total, sizes, [split])
+    top = jnp.where(mine == 0, total, other)
+    return jnp.concatenate([top, jnp.where(mine == 0, other, total)], 0)
 
 
 def in_hbm(array):
     return pltpu.with_memory_space_constraint(array, pltpu.HBM)
 
 
-def on_device(snapshots, live_rows, column_order, *, devices):
+def on_device(snapshots, live_rows, column_order, *, sizes):
     rows, width = snapshots.shape
     smem = pl.BlockSpec(memory_space=pltpu.SMEM)
     vmem = pl.BlockSpec(memory_space=pltpu.VMEM)
@@ -293,9 +302,9 @@
     params = pltpu.CompilerParams(vmem_limit_bytes=VMEM_LIMIT)
     square = jax.ShapeDtypeStruct((width, width), jnp.float32)
     tall = jax.ShapeDtypeStruct((rows, width), jnp.float32)
-    packed_rows = width + 32
+    packed_rows = width + 2 * TILE
     packed, picked = pl.pallas_call(
-        functools.partial(gram_kernel, total_rows=rows * devices),
+        functools.partial(gram_kernel, total_rows=rows * math.prod(sizes.values())),
         in_specs=[smem, hbm, hbm],
         out_specs=[vmem, vmem],
         out_shape=[jax.ShapeDtypeStruct((packed_rows, HALF), jnp.float32), tall],
@@ -306,7 +315,7 @@
         ],
         compiler_params=params,
     )(live_rows, in_hbm(column_order.reshape(1, width)), in_hbm(snapshots))
-    packed = sum_over_devices(packed, devices)
+    packed = sum_over_devices(packed, sizes)
     block = pltpu.VMEM((HALF, HALF), jnp.float32)
     return pl.pallas_call(
         finish_kernel,
@@ -330,7 +339,7 @@
 def solution(mesh):
     placed = (P(AXES, None), P(AXES), P())
     return jax.shard_map(
-        functools.partial(on_device, devices=mesh.size),
+        functools.partial(on_device, sizes={axis: mesh.shape[axis] for axis in AXES}),
         mesh=mesh,
         in_specs=placed,
         out_specs=(P(AXES, None), P(), P(AXES, None)),

time: 36.5 us -> 31.9 us (0.87)
  blocking collectives: 25.8 us -> 0 us
  waiting for transfers between devices: 0 us -> 11.7 us
  starting transfers between devices: 0 us -> 9.38 us
    all_to_all x2 -> x0, blocking collectives: 25.8 us -> none  [exchange(): return lax.all_to_all(value, AXES, 0, 0, tiled=True).reshape(shape)]
    ppermute x0 -> x7, waiting for transfers between devices: none -> 11.7 us  [flipped(): return lax.ppermute(value, axes, pairs)]
    ppermute x0 -> x7, starting transfers between devices: none -> 9.38 us  [flipped(): return lax.ppermute(value, axes, pairs)]
    pallas_call x2 -> x1, Pallas kernels: 2.64 us -> 2.6 us  [on_device(): pl.pallas_call(functools.partial(gram_kernel, total_rows=rows * math.prod...]
  transfers between devices with their start and end apart: 0 -> 7, of which waited for: 0 -> 7; matrix products, arithmetic and copies ran while one was open for 0% -> 0% of each run, Pallas kernels for 0% -> 0%
where the time goes in v4:
time: 31.9 us; the launch traced here: 31.7 us
  waiting for transfers between devices  11.7 us (37%)
  starting transfers between devices  9.38 us (29%)
  Pallas kernels  9.19 us (29%)
  between operations  1.33 us (4%)
    ppermute x7, waiting for transfers between devices, flipped(): return lax.ppermute(value, axes, pairs)  11.7 us
    ppermute x7, starting transfers between devices, flipped(): return lax.ppermute(value, axes, pairs)  9.38 us
    pallas_call x1, Pallas kernels, on_device(): pl.pallas_call(finish_kernel, in_specs=[vmem, vmem], out_specs=[hbm, hbm,...  6.59 us
    pallas_call x1, Pallas kernels, on_device(): pl.pallas_call(functools.partial(gram_kernel, total_rows=rows * math.prod...  2.6 us
  transfers between devices with their start and end apart: 7, of which 7 were waited for; matrix products, arithmetic and copies ran while one was open for 0% of the time, Pallas kernels for 0%

profile of v4, /device:TPU:0, one launch (start us, length us, event | category | flops | bytes accessed | tf_op | source)
XLA Modules:
  0.0 31.7 jit_solution(7586378584352326606)
XLA Ops:
  1.3 2.6 %shard_map.58 = (f32[272,128]{1,0:T(8,128)S(1)}, f32[1024,256]{1,0:T(8,128)S(1)}) custom-call(s32[1]{0:T(128)S(6)} %copy.6.live_ref, s32[1,256]{1,0:T(1,128)} %bitcast.8, f32[1024,256]{1,0:T(8,128)} %x_ref.1), custom_call_target="tpu_custom_call" | custom-call | tf_op jit(solution)/shard_map/pallas_call | solution.py:306
  3.9 0.5 %collective-permute-start = (f32[136,128]{1,0:T(8,128)S(1)}, f32[136,128]{1,0:T(8,128)S(1)}, u32[]{:S(2)}, u32[]{:S(2)}) collective-permute-start(f32[136,128]{1,0:T(8,128)S(1)} %dynamic-slice_bitcast_fusion), channel_id=1, source_target_pairs={{0,1},{1,0},{2,3},{3,2},{4,5},{5,4},{6,7},{7,6},{8,9},{9,8},{10,11... | collective-permute-start | bytes 208904 | tf_op jit(solution)/shard_map/ppermute | solution.py:266
  4.4 0.9 %collective-permute-done = f32[136,128]{1,0:T(8,128)S(1)} collective-permute-done((f32[136,128]{1,0:T(8,128)S(1)}, f32[136,128]{1,0:T(8,128)S(1)}, u32[]{:S(2)}, u32[]{:S(2)}) %collective-permute-start) | collective-permute-done | bytes 69664 | tf_op jit(solution)/shard_map/ppermute | solution.py:266
  5.4 3.9 %collective-permute-start.3 = (f32[136,128]{1,0:T(8,128)S(1)}, f32[136,128]{1,0:T(8,128)S(1)}, u32[]{:S(2)}, u32[]{:S(2)}) collective-permute-start(f32[136,128]{1,0:T(8,128)S(1)} %bitcast_add_fusion), channel_id=1, source_target_pairs={{0,18},{1,19},{2,16},{3,17},{16,2},{17,3},{18,0},{19,1},{4,22},{5,... | collective-permute-start | bytes 208904 | tf_op jit(solution)/shard_map/ppermute | solution.py:266
  9.2 0.5 %collective-permute-start.2 = (f32[136,128]{1,0:T(8,128)S(1)}, f32[136,128]{1,0:T(8,128)S(1)}, u32[]{:S(2)}, u32[]{:S(2)}) collective-permute-start(f32[136,128]{1,0:T(8,128)S(1)} %bitcast_add_fusion), channel_id=1, source_target_pairs={{0,2},{1,3},{2,0},{3,1},{4,6},{5,7},{6,4},{7,5},{8,10},{9,11},{10,... | collective-permute-start | bytes 208904 | tf_op jit(solution)/shard_map/ppermute | solution.py:266
  9.7 0.1 collective-permute-start.1
  9.9 2.0 %collective-permute-done.3 = f32[136,128]{1,0:T(8,128)S(1)} collective-permute-done((f32[136,128]{1,0:T(8,128)S(1)}, f32[136,128]{1,0:T(8,128)S(1)}, u32[]{:S(2)}, u32[]{:S(2)}) %collective-permute-start.3) | collective-permute-done | bytes 69664 | tf_op jit(solution)/shard_map/ppermute | solution.py:266
  11.8 1.7 %collective-permute-done.2 = f32[136,128]{1,0:T(8,128)S(1)} collective-permute-done((f32[136,128]{1,0:T(8,128)S(1)}, f32[136,128]{1,0:T(8,128)S(1)}, u32[]{:S(2)}, u32[]{:S(2)}) %collective-permute-start.2) | collective-permute-done | bytes 69664 | tf_op jit(solution)/shard_map/ppermute | solution.py:266
  13.5 0.5 %collective-permute-done.1 = f32[136,128]{1,0:T(8,128)S(1)} collective-permute-done((f32[136,128]{1,0:T(8,128)S(1)}, f32[136,128]{1,0:T(8,128)S(1)}, u32[]{:S(2)}, u32[]{:S(2)}) %collective-permute-start.1) | collective-permute-done | bytes 69664 | tf_op jit(solution)/shard_map/ppermute | solution.py:266
  14.1 1.6 %collective-permute-start.4 = (f32[136,128]{1,0:T(8,128)S(1)}, f32[136,128]{1,0:T(8,128)S(1)}, u32[]{:S(2)}, u32[]{:S(2)}) collective-permute-start(f32[136,128]{1,0:T(8,128)S(1)} %add_add_fusion), channel_id=1, source_target_pairs={{0,4},{4,0},{8,12},{12,8},{1,5},{5,1},{9,13},{13,9},{2,6},{6,2},{1... | collective-permute-start | bytes 208904 | tf_op jit(solution)/shard_map/ppermute | solution.py:266
  15.7 2.7 %collective-permute-done.4 = f32[136,128]{1,0:T(8,128)S(1)} collective-permute-done((f32[136,128]{1,0:T(8,128)S(1)}, f32[136,128]{1,0:T(8,128)S(1)}, u32[]{:S(2)}, u32[]{:S(2)}) %collective-permute-start.4) | collective-permute-done | bytes 69664 | tf_op jit(solution)/shard_map/ppermute | solution.py:266
  18.5 2.7 %collective-permute-start.5 = (f32[136,128]{1,0:T(8,128)S(1)}, f32[136,128]{1,0:T(8,128)S(1)}, u32[]{:S(2)}, u32[]{:S(2)}) collective-permute-start(f32[136,128]{1,0:T(8,128)S(1)} %add.32), channel_id=1, source_target_pairs={{0,8},{4,12},{8,0},{12,4},{1,9},{5,13},{9,1},{13,5},{2,10},{6,14},... | collective-permute-start | bytes 208904 | tf_op jit(solution)/shard_map/ppermute | solution.py:266
  21.1 2.6 %collective-permute-done.5 = f32[136,128]{1,0:T(8,128)S(1)} collective-permute-done((f32[136,128]{1,0:T(8,128)S(1)}, f32[136,128]{1,0:T(8,128)S(1)}, u32[]{:S(2)}, u32[]{:S(2)}) %collective-permute-start.5) | collective-permute-done | bytes 69664 | tf_op jit(solution)/shard_map/ppermute | solution.py:266
  23.8 0.1 collective-permute-start.6
  23.8 1.2 %collective-permute-done.6 = f32[136,128]{1,0:T(8,128)S(1)} collective-permute-done((f32[136,128]{1,0:T(8,128)S(1)}, f32[136,128]{1,0:T(8,128)S(1)}, u32[]{:S(2)}, u32[]{:S(2)}) %collective-permute-start.6) | collective-permute-done | bytes 69664 | tf_op jit(solution)/shard_map/ppermute | solution.py:266
  25.1 6.6 %shard_map.59 = (f32[1024,256]{1,0:T(8,128)}, f32[256,256]{1,0:T(8,128)}, f32[1024,256]{1,0:T(8,128)}) custom-call(f32[272,128]{1,0:T(8,128)S(1)} %pad_maximum_fusion.packed_ref, f32[1024,256]{1,0:T(8,128)S(1)} %get-tuple-element.6.picked_ref), custom_call_target="tpu_custom_call" | custom-call | tf_op jit(solution)/shard_map/pallas_call | solution.py:320
  (7 shorter events, 0.1 us)
Async XLA Ops:
  3.9 1.4 %collective-permute-start = (f32[136,128]{1,0:T(8,128)S(1)}, f32[136,128]{1,0:T(8,128)S(1)}, u32[]{:S(2)}, u32[]{:S(2)}) collective-permute-start(f32[136,128]{1,0:T(8,128)S(1)} %dynamic-slice_bitcast_fusion), channel_id=1, source_target_pairs={{0,1},{1,0},{2,3},{3,2},{4,5},{5,4},{6,7},{7,6},{8,9},{9,8},{10,11... | collective-permute-start | bytes 208904 | tf_op jit(solution)/shard_map/ppermute | solution.py:266
  5.4 6.5 %collective-permute-start.3 = (f32[136,128]{1,0:T(8,128)S(1)}, f32[136,128]{1,0:T(8,128)S(1)}, u32[]{:S(2)}, u32[]{:S(2)}) collective-permute-start(f32[136,128]{1,0:T(8,128)S(1)} %bitcast_add_fusion), channel_id=1, source_target_pairs={{0,18},{1,19},{2,16},{3,17},{16,2},{17,3},{18,0},{19,1},{4,22},{5,... | collective-permute-start | bytes 208904 | tf_op jit(solution)/shard_map/ppermute | solution.py:266
  9.2 4.3 %collective-permute-start.2 = (f32[136,128]{1,0:T(8,128)S(1)}, f32[136,128]{1,0:T(8,128)S(1)}, u32[]{:S(2)}, u32[]{:S(2)}) collective-permute-start(f32[136,128]{1,0:T(8,128)S(1)} %bitcast_add_fusion), channel_id=1, source_target_pairs={{0,2},{1,3},{2,0},{3,1},{4,6},{5,7},{6,4},{7,5},{8,10},{9,11},{10,... | collective-permute-start | bytes 208904 | tf_op jit(solution)/shard_map/ppermute | solution.py:266
  9.7 4.3 %collective-permute-start.1 = (f32[136,128]{1,0:T(8,128)S(1)}, f32[136,128]{1,0:T(8,128)S(1)}, u32[]{:S(2)}, u32[]{:S(2)}) collective-permute-start(f32[136,128]{1,0:T(8,128)S(1)} %bitcast_add_fusion), channel_id=1, source_target_pairs={{0,16},{16,0},{1,17},{17,1},{2,18},{18,2},{3,19},{19,3},{4,20},{20... | collective-permute-start | bytes 208904 | tf_op jit(solution)/shard_map/ppermute | solution.py:266
  14.1 4.4 %collective-permute-start.4 = (f32[136,128]{1,0:T(8,128)S(1)}, f32[136,128]{1,0:T(8,128)S(1)}, u32[]{:S(2)}, u32[]{:S(2)}) collective-permute-start(f32[136,128]{1,0:T(8,128)S(1)} %add_add_fusion), channel_id=1, source_target_pairs={{0,4},{4,0},{8,12},{12,8},{1,5},{5,1},{9,13},{13,9},{2,6},{6,2},{1... | collective-permute-start | bytes 208904 | tf_op jit(solution)/shard_map/ppermute | solution.py:266
  18.5 5.3 %collective-permute-start.5 = (f32[136,128]{1,0:T(8,128)S(1)}, f32[136,128]{1,0:T(8,128)S(1)}, u32[]{:S(2)}, u32[]{:S(2)}) collective-permute-start(f32[136,128]{1,0:T(8,128)S(1)} %add.32), channel_id=1, source_target_pairs={{0,8},{4,12},{8,0},{12,4},{1,9},{5,13},{9,1},{13,5},{2,10},{6,14},... | collective-permute-start | bytes 208904 | tf_op jit(solution)/shard_map/ppermute | solution.py:266
  23.8 1.3 %collective-permute-start.6 = (f32[136,128]{1,0:T(8,128)S(1)}, f32[136,128]{1,0:T(8,128)S(1)}, u32[]{:S(2)}, u32[]{:S(2)}) collective-permute-start(f32[136,128]{1,0:T(8,128)S(1)} %add.33), channel_id=1, source_target_pairs={{0,1},{1,0},{2,3},{3,2},{4,5},{5,4},{6,7},{7,6},{8,9},{9,8},{10,11... | collective-permute-start | bytes 208904 | tf_op jit(solution)/shard_map/ppermute | solution.py:266

commit v5 on v3

--- a/solution.py
+++ b/solution.py
@@ -15,6 +15,7 @@
 VMEM_LIMIT = 16 * 1024 * 1024
 LOADS = 2
 PIECES = 8
+LAST = 4
 
 
 def dot(a, b, dims=((1,), (0,)), precision=None):
@@ -79,16 +80,6 @@
     packed_ref[2 * HALF : 2 * HALF + 1] = jnp.sum(jnp.where(i == j, last, 0.0), 0, keepdims=True)
 
 
-def sum_kernel(parts_ref, out_ref, *, devices):
-    each = parts_ref.shape[0] // devices
-    terms = [parts_ref[k * each : (k + 1) * each] for k in range(devices)]
-    while len(terms) > 1:
-        pairs = [a + b for a, b in zip(terms[::2], terms[1::2])]
-        terms = pairs + terms[len(pairs) * 2 :]
-    for k in range(devices):
-        out_ref[k * each : (k + 1) * each] = terms[0]
-
-
 def spread(value):
     return jnp.broadcast_to(value, (TILE, HALF))
 
@@ -135,34 +126,28 @@
         for m in range(width):
             home, at = divmod(m, TILE)
             here = subs == at
-            pivot = spread(column[m][home][at : at + 1])
-            recip = 1.0 / pivot
-            root = lax.rsqrt(pivot)
+            recip = 1.0 / spread(column[m][home][at : at + 1])
             times = list(column[m])
             times[home] = jnp.where(here, 0.0, times[home])
             times = [value * recip for value in times]
             for q in range(m + 1, width):
                 value = spread(column[q][home][at : at + 1])
                 column[q] = [c - t * value for c, t in zip(column[q], times)]
-            row_up = spread(panel[home][at : at + 1]) * root
             lane = lanes == first + m
+            up[home] = jnp.where(here, panel[home], up[home]) if at else panel[home]
             panel = [
                 jnp.where(lane, jnp.where(here, 1.0, 0.0) if h == home else 0.0, panel[h])
                 for h in range(WIDE)
             ]
+            low[home] = jnp.where(here, panel[home], low[home]) if at else panel[home]
+            scale[home] = jnp.where(here, recip, scale[home]) if at else recip
             row = spread(panel[home][at : at + 1])
-            row_low = row * root
-            if at:
-                up[home] = jnp.where(here, row_up, up[home])
-                low[home] = jnp.where(here, row_low, low[home])
-                scale[home] = jnp.where(here, recip, scale[home])
-            else:
-                up[home], low[home], scale[home] = row_up, row_low, recip
             panel = [p - t * row for p, t in zip(panel, times)]
         for h, g in enumerate(mine):
             at = slice(g * TILE, (g + 1) * TILE)
-            upper_ref[at] = jnp.where(lanes >= subs + g * TILE, up[h], 0.0)
-            inverse_ref[at] = jnp.where(lanes <= subs + g * TILE, low[h], 0.0)
+            root = scale[h] * lax.rsqrt(scale[h])
+            upper_ref[at] = jnp.where(lanes >= subs + g * TILE, up[h] * root, 0.0)
+            inverse_ref[at] = jnp.where(lanes <= subs + g * TILE, low[h] * root, 0.0)
         inside = (lanes >= first) & (lanes < first + width)
         solved = [p * c for p, c in zip(panel, scale)]
         for g in near:
@@ -253,7 +238,8 @@
     tri[HALF:, HALF:] = upper[...]
     send(tri, tri_ref, pl.ds(0, 2 * HALF), all_lanes)
     to_right = inverse_weights()
-    for s in range(PIECES):
+    chunk = rows // LAST
+    for s in range(LAST):
         at = slice(s * chunk, (s + 1) * chunk)
         rh, rl = halves(rest[at])
         basis[at, HALF:] = fold(dot(jnp.concatenate([rh, rl], 1), to_right, ((1,), (1,))))
@@ -263,22 +249,31 @@
 
 
 def sum_over_devices(packed, devices):
-    if packed.shape[0] % devices:
+    if devices & (devices - 1) or devices < 32:
         return lax.psum(packed, AXES)
-    shape = packed.shape
-
-    def exchange(value):
-        value = value.reshape(shape[0], 1, shape[1])
-        return lax.all_to_all(value, AXES, 0, 0, tiled=True).reshape(shape)
-
-    total = pl.pallas_call(
-        functools.partial(sum_kernel, devices=devices),
-        in_specs=[pl.BlockSpec(memory_space=pltpu.VMEM)],
-        out_specs=pl.BlockSpec(memory_space=pltpu.VMEM),
-        out_shape=jax.ShapeDtypeStruct(shape, jnp.float32),
-        compiler_params=pltpu.CompilerParams(vmem_limit_bytes=VMEM_LIMIT),
-    )(exchange(packed))
-    return exchange(total)
+
+    def flip(value, masks):
+        pairs = [(i, i ^ masks[i & 1]) for i in range(devices)]
+        return lax.ppermute(value, AXES, pairs)
+
+    def add_four(value, one, two):
+        both = tuple(a ^ b for a, b in zip(one, two))
+        first, second, third = flip(value, one), flip(value, two), flip(value, both)
+        return (value + first) + (second + third)
+
+    half = packed.shape[0] // 2
+    mine = lax.axis_index(AXES) & 1
+    parts = packed.reshape(2, half, packed.shape[1])
+    total = lax.dynamic_index_in_dim(parts, mine, 0, False) + flip(
+        lax.dynamic_index_in_dim(parts, 1 - mine, 0, False), (1, 1)
+    )
+    total = add_four(total, (2, 16), (8, 4))
+    total = add_four(total, (16, 2), (4, 8))
+    for bit in range(5, devices.bit_length() - 1):
+        total = total + flip(total, (1 << bit, 1 << bit))
+    other = flip(total, (1, 1))
+    top = jnp.where(mine == 0, total, other)
+    return jnp.concatenate([top, jnp.where(mine == 0, other, total)], 0)
 
 
 def in_hbm(array):
@@ -293,7 +288,7 @@
     params = pltpu.CompilerParams(vmem_limit_bytes=VMEM_LIMIT)
     square = jax.ShapeDtypeStruct((width, width), jnp.float32)
     tall = jax.ShapeDtypeStruct((rows, width), jnp.float32)
-    packed_rows = width + 32
+    packed_rows = width + 2 * TILE
     packed, picked = pl.pallas_call(
         functools.partial(gram_kernel, total_rows=rows * devices),
         in_specs=[smem, hbm, hbm],
@@ -321,7 +316,7 @@
             block,
             block,
             block,
-            pltpu.SemaphoreType.DMA((3 * PIECES + 1,)),
+            pltpu.SemaphoreType.DMA((2 * PIECES + LAST + 1,)),
         ],
         compiler_params=params,
     )(packed, picked)

time: 36.5 us -> 30.9 us (0.85)
  blocking collectives: 25.8 us -> 0 us
  waiting for transfers between devices: 0 us -> 10.5 us
  starting transfers between devices: 0 us -> 9.71 us
    all_to_all x2 -> x0, blocking collectives: 25.8 us -> none  [exchange(): return lax.all_to_all(value, AXES, 0, 0, tiled=True).reshape(shape)]
    ppermute x0 -> x8, waiting for transfers between devices: none -> 10.5 us  [flip(): return lax.ppermute(value, AXES, pairs)]
    ppermute x0 -> x8, starting transfers between devices: none -> 9.71 us  [flip(): return lax.ppermute(value, AXES, pairs)]
  transfers between devices with their start and end apart: 0 -> 8, of which waited for: 0 -> 7; matrix products, arithmetic and copies ran while one was open for 0% -> 0% of each run, Pallas kernels for 0% -> 0%
where the time goes in v5:
time: 30.9 us; the launch traced here: 30.7 us
  waiting for transfers between devices  10.5 us (34%)
  starting transfers between devices  9.71 us (31%)
  Pallas kernels  9.07 us (29%)
  between operations  1.34 us (4%)
    ppermute x8, waiting for transfers between devices, flip(): return lax.ppermute(value, AXES, pairs)  10.5 us
    ppermute x8, starting transfers between devices, flip(): return lax.ppermute(value, AXES, pairs)  9.71 us
    pallas_call x1, Pallas kernels, on_device(): pl.pallas_call(finish_kernel, in_specs=[vmem, vmem], out_specs=[hbm, hbm,...  6.46 us
    pallas_call x1, Pallas kernels, on_device(): pl.pallas_call(functools.partial(gram_kernel, total_rows=rows * devices),...  2.61 us
  transfers between devices with their start and end apart: 8, of which 7 were waited for; matrix products, arithmetic and copies ran while one was open for 0% of the time, Pallas kernels for 0%

profile of v5, /device:TPU:0, one launch (start us, length us, event | category | flops | bytes accessed | tf_op | source)
XLA Modules:
  0.0 30.7 jit_solution(15269078907354384343)
XLA Ops:
  1.3 2.6 %shard_map.58 = (f32[272,128]{1,0:T(8,128)S(1)}, f32[1024,256]{1,0:T(8,128)S(1)}) custom-call(s32[1]{0:T(128)S(6)} %copy.6.live_ref, s32[1,256]{1,0:T(1,128)} %bitcast.8, f32[1024,256]{1,0:T(8,128)} %x_ref.1), custom_call_target="tpu_custom_call" | custom-call | tf_op jit(solution)/shard_map/pallas_call | solution.py:292
  3.9 0.5 %collective-permute-start = (f32[136,128]{1,0:T(8,128)S(1)}, f32[136,128]{1,0:T(8,128)S(1)}, u32[]{:S(2)}, u32[]{:S(2)}) collective-permute-start(f32[136,128]{1,0:T(8,128)S(1)} %dynamic-slice_bitcast_fusion), channel_id=1, source_target_pairs={{0,1},{1,0},{2,3},{3,2},{4,5},{5,4},{6,7},{7,6},{8,9},{9,8},{10,11... | collective-permute-start | bytes 208904 | tf_op jit(solution)/shard_map/ppermute | solution.py:257
  4.4 0.9 %collective-permute-done = f32[136,128]{1,0:T(8,128)S(1)} collective-permute-done((f32[136,128]{1,0:T(8,128)S(1)}, f32[136,128]{1,0:T(8,128)S(1)}, u32[]{:S(2)}, u32[]{:S(2)}) %collective-permute-start) | collective-permute-done | bytes 69664 | tf_op jit(solution)/shard_map/ppermute | solution.py:257
  5.4 4.9 %collective-permute-start.3 = (f32[136,128]{1,0:T(8,128)S(1)}, f32[136,128]{1,0:T(8,128)S(1)}, u32[]{:S(2)}, u32[]{:S(2)}) collective-permute-start(f32[136,128]{1,0:T(8,128)S(1)} %bitcast_add_fusion), channel_id=1, source_target_pairs={{0,10},{1,21},{2,8},{3,23},{4,14},{5,17},{6,12},{7,19},{8,2},{9,29... | collective-permute-start | bytes 208904 | tf_op jit(solution)/shard_map/ppermute | solution.py:257
  10.3 0.3 %collective-permute-start.2 = (f32[136,128]{1,0:T(8,128)S(1)}, f32[136,128]{1,0:T(8,128)S(1)}, u32[]{:S(2)}, u32[]{:S(2)}) collective-permute-start(f32[136,128]{1,0:T(8,128)S(1)} %bitcast_add_fusion), channel_id=1, source_target_pairs={{0,8},{1,5},{2,10},{3,7},{4,12},{5,1},{6,14},{7,3},{8,0},{9,13},{1... | collective-permute-start | bytes 208904 | tf_op jit(solution)/shard_map/ppermute | solution.py:257
  10.6 0.3 %collective-permute-start.1 = (f32[136,128]{1,0:T(8,128)S(1)}, f32[136,128]{1,0:T(8,128)S(1)}, u32[]{:S(2)}, u32[]{:S(2)}) collective-permute-start(f32[136,128]{1,0:T(8,128)S(1)} %bitcast_add_fusion), channel_id=1, source_target_pairs={{0,2},{1,17},{2,0},{3,19},{4,6},{5,21},{6,4},{7,23},{8,10},{9,25},... | collective-permute-start | bytes 208904 | tf_op jit(solution)/shard_map/ppermute | solution.py:257
  10.9 1.7 %collective-permute-done.3 = f32[136,128]{1,0:T(8,128)S(1)} collective-permute-done((f32[136,128]{1,0:T(8,128)S(1)}, f32[136,128]{1,0:T(8,128)S(1)}, u32[]{:S(2)}, u32[]{:S(2)}) %collective-permute-start.3) | collective-permute-done | bytes 69664 | tf_op jit(solution)/shard_map/ppermute | solution.py:257
  12.7 2.8 %collective-permute-done.2 = f32[136,128]{1,0:T(8,128)S(1)} collective-permute-done((f32[136,128]{1,0:T(8,128)S(1)}, f32[136,128]{1,0:T(8,128)S(1)}, u32[]{:S(2)}, u32[]{:S(2)}) %collective-permute-start.2) | collective-permute-done | bytes 69664 | tf_op jit(solution)/shard_map/ppermute | solution.py:257
  15.5 0.0 collective-permute-done.1
  15.5 2.6 %collective-permute-start.6 = (f32[136,128]{1,0:T(8,128)S(1)}, f32[136,128]{1,0:T(8,128)S(1)}, u32[]{:S(2)}, u32[]{:S(2)}) collective-permute-start(f32[136,128]{1,0:T(8,128)S(1)} %add_add_fusion.1), channel_id=1, source_target_pairs={{0,20},{1,11},{2,22},{3,9},{4,16},{5,15},{6,18},{7,13},{8,28},{9,3... | collective-permute-start | bytes 208904 | tf_op jit(solution)/shard_map/ppermute | solution.py:257
  18.1 0.4 %collective-permute-start.5 = (f32[136,128]{1,0:T(8,128)S(1)}, f32[136,128]{1,0:T(8,128)S(1)}, u32[]{:S(2)}, u32[]{:S(2)}) collective-permute-start(f32[136,128]{1,0:T(8,128)S(1)} %add_add_fusion.1), channel_id=1, source_target_pairs={{0,4},{1,9},{2,6},{3,11},{4,0},{5,13},{6,2},{7,15},{8,12},{9,1},{1... | collective-permute-start | bytes 208904 | tf_op jit(solution)/shard_map/ppermute | solution.py:257
  18.6 0.5 %collective-permute-start.4 = (f32[136,128]{1,0:T(8,128)S(1)}, f32[136,128]{1,0:T(8,128)S(1)}, u32[]{:S(2)}, u32[]{:S(2)}) collective-permute-start(f32[136,128]{1,0:T(8,128)S(1)} %add_add_fusion.1), channel_id=1, source_target_pairs={{0,16},{1,3},{2,18},{3,1},{4,20},{5,7},{6,22},{7,5},{8,24},{9,11},... | collective-permute-start | bytes 208904 | tf_op jit(solution)/shard_map/ppermute | solution.py:257
  19.1 2.3 %collective-permute-done.6 = f32[136,128]{1,0:T(8,128)S(1)} collective-permute-done((f32[136,128]{1,0:T(8,128)S(1)}, f32[136,128]{1,0:T(8,128)S(1)}, u32[]{:S(2)}, u32[]{:S(2)}) %collective-permute-start.6) | collective-permute-done | bytes 69664 | tf_op jit(solution)/shard_map/ppermute | solution.py:257
  21.4 1.1 %collective-permute-done.5 = f32[136,128]{1,0:T(8,128)S(1)} collective-permute-done((f32[136,128]{1,0:T(8,128)S(1)}, f32[136,128]{1,0:T(8,128)S(1)}, u32[]{:S(2)}, u32[]{:S(2)}) %collective-permute-start.5) | collective-permute-done | bytes 69664 | tf_op jit(solution)/shard_map/ppermute | solution.py:257
  22.4 0.4 %collective-permute-done.4 = f32[136,128]{1,0:T(8,128)S(1)} collective-permute-done((f32[136,128]{1,0:T(8,128)S(1)}, f32[136,128]{1,0:T(8,128)S(1)}, u32[]{:S(2)}, u32[]{:S(2)}) %collective-permute-start.4) | collective-permute-done | bytes 69664 | tf_op jit(solution)/shard_map/ppermute | solution.py:257
  22.9 0.1 collective-permute-start.7
  23.0 1.2 %collective-permute-done.7 = f32[136,128]{1,0:T(8,128)S(1)} collective-permute-done((f32[136,128]{1,0:T(8,128)S(1)}, f32[136,128]{1,0:T(8,128)S(1)}, u32[]{:S(2)}, u32[]{:S(2)}) %collective-permute-start.7) | collective-permute-done | bytes 69664 | tf_op jit(solution)/shard_map/ppermute | solution.py:257
  24.3 6.5 %shard_map.59 = (f32[1024,256]{1,0:T(8,128)}, f32[256,256]{1,0:T(8,128)}, f32[1024,256]{1,0:T(8,128)}) custom-call(f32[272,128]{1,0:T(8,128)S(1)} %pad_maximum_fusion.packed_ref, f32[1024,256]{1,0:T(8,128)S(1)} %get-tuple-element.6.picked_ref), custom_call_target="tpu_custom_call" | custom-call | tf_op jit(solution)/shard_map/pallas_call | solution.py:306
  (6 shorter events, 0.1 us)
Async XLA Ops:
  3.9 1.4 %collective-permute-start = (f32[136,128]{1,0:T(8,128)S(1)}, f32[136,128]{1,0:T(8,128)S(1)}, u32[]{:S(2)}, u32[]{:S(2)}) collective-permute-start(f32[136,128]{1,0:T(8,128)S(1)} %dynamic-slice_bitcast_fusion), channel_id=1, source_target_pairs={{0,1},{1,0},{2,3},{3,2},{4,5},{5,4},{6,7},{7,6},{8,9},{9,8},{10,11... | collective-permute-start | bytes 208904 | tf_op jit(solution)/shard_map/ppermute | solution.py:257
  5.4 7.3 %collective-permute-start.3 = (f32[136,128]{1,0:T(8,128)S(1)}, f32[136,128]{1,0:T(8,128)S(1)}, u32[]{:S(2)}, u32[]{:S(2)}) collective-permute-start(f32[136,128]{1,0:T(8,128)S(1)} %bitcast_add_fusion), channel_id=1, source_target_pairs={{0,10},{1,21},{2,8},{3,23},{4,14},{5,17},{6,12},{7,19},{8,2},{9,29... | collective-permute-start | bytes 208904 | tf_op jit(solution)/shard_map/ppermute | solution.py:257
  10.3 5.2 %collective-permute-start.2 = (f32[136,128]{1,0:T(8,128)S(1)}, f32[136,128]{1,0:T(8,128)S(1)}, u32[]{:S(2)}, u32[]{:S(2)}) collective-permute-start(f32[136,128]{1,0:T(8,128)S(1)} %bitcast_add_fusion), channel_id=1, source_target_pairs={{0,8},{1,5},{2,10},{3,7},{4,12},{5,1},{6,14},{7,3},{8,0},{9,13},{1... | collective-permute-start | bytes 208904 | tf_op jit(solution)/shard_map/ppermute | solution.py:257
  10.6 4.9 %collective-permute-start.1 = (f32[136,128]{1,0:T(8,128)S(1)}, f32[136,128]{1,0:T(8,128)S(1)}, u32[]{:S(2)}, u32[]{:S(2)}) collective-permute-start(f32[136,128]{1,0:T(8,128)S(1)} %bitcast_add_fusion), channel_id=1, source_target_pairs={{0,2},{1,17},{2,0},{3,19},{4,6},{5,21},{6,4},{7,23},{8,10},{9,25},... | collective-permute-start | bytes 208904 | tf_op jit(solution)/shard_map/ppermute | solution.py:257
  15.5 5.8 %collective-permute-start.6 = (f32[136,128]{1,0:T(8,128)S(1)}, f32[136,128]{1,0:T(8,128)S(1)}, u32[]{:S(2)}, u32[]{:S(2)}) collective-permute-start(f32[136,128]{1,0:T(8,128)S(1)} %add_add_fusion.1), channel_id=1, source_target_pairs={{0,20},{1,11},{2,22},{3,9},{4,16},{5,15},{6,18},{7,13},{8,28},{9,3... | collective-permute-start | bytes 208904 | tf_op jit(solution)/shard_map/ppermute | solution.py:257
  18.1 4.3 %collective-permute-start.5 = (f32[136,128]{1,0:T(8,128)S(1)}, f32[136,128]{1,0:T(8,128)S(1)}, u32[]{:S(2)}, u32[]{:S(2)}) collective-permute-start(f32[136,128]{1,0:T(8,128)S(1)} %add_add_fusion.1), channel_id=1, source_target_pairs={{0,4},{1,9},{2,6},{3,11},{4,0},{5,13},{6,2},{7,15},{8,12},{9,1},{1... | collective-permute-start | bytes 208904 | tf_op jit(solution)/shard_map/ppermute | solution.py:257
  18.6 4.3 %collective-permute-start.4 = (f32[136,128]{1,0:T(8,128)S(1)}, f32[136,128]{1,0:T(8,128)S(1)}, u32[]{:S(2)}, u32[]{:S(2)}) collective-permute-start(f32[136,128]{1,0:T(8,128)S(1)} %add_add_fusion.1), channel_id=1, source_target_pairs={{0,16},{1,3},{2,18},{3,1},{4,20},{5,7},{6,22},{7,5},{8,24},{9,11},... | collective-permute-start | bytes 208904 | tf_op jit(solution)/shard_map/ppermute | solution.py:257
  22.9 1.3 %collective-permute-start.7 = (f32[136,128]{1,0:T(8,128)S(1)}, f32[136,128]{1,0:T(8,128)S(1)}, u32[]{:S(2)}, u32[]{:S(2)}) collective-permute-start(f32[136,128]{1,0:T(8,128)S(1)} %add_add_fusion), channel_id=1, source_target_pairs={{0,1},{1,0},{2,3},{3,2},{4,5},{5,4},{6,7},{7,6},{8,9},{9,8},{10,11... | collective-permute-start | bytes 208904 | tf_op jit(solution)/shard_map/ppermute | solution.py:257

commit v6 on v5

--- a/solution.py
+++ b/solution.py
@@ -13,7 +13,7 @@
 WIDE = 2
 AXES = ("lon", "lat", "depth")
 VMEM_LIMIT = 16 * 1024 * 1024
-LOADS = 2
+LOADS = 1
 PIECES = 8
 LAST = 4
 
@@ -43,7 +43,7 @@
 
 
 def gram_kernel(
-    live_ref, order_in, x_ref, packed_ref, picked_ref, held, order_ref, sems, *, total_rows
+    live_ref, order_in, x_ref, packed_ref, high_ref, low_ref, held, order_ref, sems, *, total_rows
 ):
     rows, width = held.shape
     chunk = rows // LOADS
@@ -58,19 +58,18 @@
     pick = one_hot(order_ref)
     both = jnp.zeros((width, width), jnp.float32)
     cross = jnp.zeros((width, width), jnp.float32)
+    down = ((0,), (0,))
     for c in range(LOADS):
         at = slice(c * chunk, (c + 1) * chunk)
         copies[c].wait()
         row = lax.broadcasted_iota(jnp.int32, (chunk, width), 0) + c * chunk
-        x = jnp.where(row < live_ref[0], held[at], 0.0)
-        high, middle, low = (dot(part, pick) for part in thirds(x))
-        picked_ref[at] = high + (middle + low)
-        high = high.astype(jnp.bfloat16)
-        middle = middle.astype(jnp.bfloat16)
-        low = low.astype(jnp.bfloat16)
-        down = ((0,), (0,))
-        both = both + (dot(high, high, down) + dot(middle, middle, down))
-        cross = cross + (dot(high, middle, down) + dot(high, low, down))
+        high, low = halves(jnp.where(row < live_ref[0], held[at], 0.0))
+        high = dot(high, pick).astype(jnp.bfloat16)
+        low = dot(low, pick).astype(jnp.bfloat16)
+        high_ref[at] = high
+        low_ref[at] = low
+        both = both + (dot(high, high, down) + dot(low, low, down))
+        cross = cross + dot(high, low, down)
     gram = (both + (cross + cross.T)) / total_rows
     i, j = square_iotas()
     packed_ref[:HALF] = gram[:HALF, HALF:]
@@ -171,10 +170,10 @@
 
 
 def finish_kernel(
-    packed_ref, picked_ref, basis_ref, tri_ref, high_ref,
+    packed_ref, xh_ref, xl_ref, basis_ref, tri_ref, high_ref,
     basis, tri, high, rest, upper, inverse, update, sems,
 ):
-    rows = picked_ref.shape[0]
+    rows = xh_ref.shape[0]
     chunk = rows // PIECES
     i, j = square_iotas()
     mixed = packed_ref[HALF : 2 * HALF]
@@ -223,13 +222,14 @@
 
     def first_half(s):
         at = slice(s * chunk, (s + 1) * chunk)
-        xh, xl = halves(picked_ref[at, :HALF])
-        left = fold(dot(jnp.concatenate([xh, xl], 1), to_left, ((1,), (1,))))
+        xh, xl = xh_ref[at], xl_ref[at]
+        left = fold(dot(jnp.concatenate([xh[:, :HALF], xl[:, :HALF]], 1), to_left, ((1,), (1,))))
+        x = xh.astype(jnp.float32) + xl.astype(jnp.float32)
         basis[at, :HALF] = left
         lh, ll = halves(left)
         both = jnp.concatenate([lh, ll], 1)
-        rest[at] = picked_ref[at, HALF:] - fold(dot(both, to_rest))
-        high[at] = picked_ref[at] - (dot(both, to_high) + dot(lh, to_high_low))
+        rest[at] = x[:, HALF:] - fold(dot(both, to_rest))
+        high[at] = x - (dot(both, to_high) + dot(lh, to_high_low))
         rows_at = pl.ds(s * chunk, chunk)
         send(basis, basis_ref, rows_at, left_lanes)
         send(high, high_ref, rows_at, all_lanes)
@@ -288,12 +288,13 @@
     params = pltpu.CompilerParams(vmem_limit_bytes=VMEM_LIMIT)
     square = jax.ShapeDtypeStruct((width, width), jnp.float32)
     tall = jax.ShapeDtypeStruct((rows, width), jnp.float32)
+    part = jax.ShapeDtypeStruct((rows, width), jnp.bfloat16)
     packed_rows = width + 2 * TILE
-    packed, picked = pl.pallas_call(
+    packed, xh, xl = pl.pallas_call(
         functools.partial(gram_kernel, total_rows=rows * devices),
         in_specs=[smem, hbm, hbm],
-        out_specs=[vmem, vmem],
-        out_shape=[jax.ShapeDtypeStruct((packed_rows, HALF), jnp.float32), tall],
+        out_specs=[vmem, vmem, vmem],
+        out_shape=[jax.ShapeDtypeStruct((packed_rows, HALF), jnp.float32), part, part],
         scratch_shapes=[
             pltpu.VMEM((rows, width), jnp.float32),
             pltpu.VMEM((1, width), jnp.int32),
@@ -305,7 +306,7 @@
     block = pltpu.VMEM((HALF, HALF), jnp.float32)
     return pl.pallas_call(
         finish_kernel,
-        in_specs=[vmem, vmem],
+        in_specs=[vmem, vmem, vmem],
         out_specs=[hbm, hbm, hbm],
         out_shape=[tall, square, tall],
         scratch_shapes=[
@@ -319,7 +320,7 @@
             pltpu.SemaphoreType.DMA((2 * PIECES + LAST + 1,)),
         ],
         compiler_params=params,
-    )(packed, picked)
+    )(packed, xh, xl)
 
 
 def solution(mesh):

time: 30.9 us -> 30.6 us (level)
  no operation moved by 1% of the time
where the time goes in v6:
time: 30.6 us; the launch traced here: 30.5 us
  waiting for transfers between devices  10.5 us (34%)
  starting transfers between devices  9.72 us (32%)
  Pallas kernels  8.83 us (29%)
  between operations  1.34 us (4%)
    ppermute x8, waiting for transfers between devices, flip(): return lax.ppermute(value, AXES, pairs)  10.5 us
    ppermute x8, starting transfers between devices, flip(): return lax.ppermute(value, AXES, pairs)  9.72 us
    pallas_call x1, Pallas kernels, on_device(): pl.pallas_call(finish_kernel, in_specs=[vmem, vmem, vmem], out_specs=[hbm...  6.46 us
    pallas_call x1, Pallas kernels, on_device(): pl.pallas_call(functools.partial(gram_kernel, total_rows=rows * devices),...  2.38 us
  transfers between devices with their start and end apart: 8, of which 7 were waited for; matrix products, arithmetic and copies ran while one was open for 0% of the time, Pallas kernels for 0%

profile of v6, /device:TPU:0, one launch (start us, length us, event | category | flops | bytes accessed | tf_op | source)
XLA Modules:
  0.0 30.5 jit_solution(15521820151333332431)
XLA Ops:
  1.3 2.4 %shard_map.58 = (f32[272,128]{1,0:T(8,128)S(1)}, bf16[1024,256]{1,0:T(8,128)(2,1)S(1)}, bf16[1024,256]{1,0:T(8,128)(2,1)S(1)}) custom-call(s32[1]{0:T(128)S(6)} %copy.6.live_ref, s32[1,256]{1,0:T(1,128)} %bitcast.8, f32[1024,256]{1,0:T(8,128)} %x_ref.1), custom_call_target="tpu_custom_call" | custom-call | tf_op jit(solution)/shard_map/pallas_call | solution.py:293
  3.7 0.5 %collective-permute-start = (f32[136,128]{1,0:T(8,128)S(1)}, f32[136,128]{1,0:T(8,128)S(1)}, u32[]{:S(2)}, u32[]{:S(2)}) collective-permute-start(f32[136,128]{1,0:T(8,128)S(1)} %dynamic-slice_bitcast_fusion), channel_id=1, source_target_pairs={{0,1},{1,0},{2,3},{3,2},{4,5},{5,4},{6,7},{7,6},{8,9},{9,8},{10,11... | collective-permute-start | bytes 208904 | tf_op jit(solution)/shard_map/ppermute | solution.py:257
  4.2 0.9 %collective-permute-done = f32[136,128]{1,0:T(8,128)S(1)} collective-permute-done((f32[136,128]{1,0:T(8,128)S(1)}, f32[136,128]{1,0:T(8,128)S(1)}, u32[]{:S(2)}, u32[]{:S(2)}) %collective-permute-start) | collective-permute-done | bytes 69664 | tf_op jit(solution)/shard_map/ppermute | solution.py:257
  5.1 4.9 %collective-permute-start.3 = (f32[136,128]{1,0:T(8,128)S(1)}, f32[136,128]{1,0:T(8,128)S(1)}, u32[]{:S(2)}, u32[]{:S(2)}) collective-permute-start(f32[136,128]{1,0:T(8,128)S(1)} %bitcast_add_fusion), channel_id=1, source_target_pairs={{0,10},{1,21},{2,8},{3,23},{4,14},{5,17},{6,12},{7,19},{8,2},{9,29... | collective-permute-start | bytes 208904 | tf_op jit(solution)/shard_map/ppermute | solution.py:257
  10.1 0.3 %collective-permute-start.2 = (f32[136,128]{1,0:T(8,128)S(1)}, f32[136,128]{1,0:T(8,128)S(1)}, u32[]{:S(2)}, u32[]{:S(2)}) collective-permute-start(f32[136,128]{1,0:T(8,128)S(1)} %bitcast_add_fusion), channel_id=1, source_target_pairs={{0,8},{1,5},{2,10},{3,7},{4,12},{5,1},{6,14},{7,3},{8,0},{9,13},{1... | collective-permute-start | bytes 208904 | tf_op jit(solution)/shard_map/ppermute | solution.py:257
  10.4 0.3 %collective-permute-start.1 = (f32[136,128]{1,0:T(8,128)S(1)}, f32[136,128]{1,0:T(8,128)S(1)}, u32[]{:S(2)}, u32[]{:S(2)}) collective-permute-start(f32[136,128]{1,0:T(8,128)S(1)} %bitcast_add_fusion), channel_id=1, source_target_pairs={{0,2},{1,17},{2,0},{3,19},{4,6},{5,21},{6,4},{7,23},{8,10},{9,25},... | collective-permute-start | bytes 208904 | tf_op jit(solution)/shard_map/ppermute | solution.py:257
  10.7 1.7 %collective-permute-done.3 = f32[136,128]{1,0:T(8,128)S(1)} collective-permute-done((f32[136,128]{1,0:T(8,128)S(1)}, f32[136,128]{1,0:T(8,128)S(1)}, u32[]{:S(2)}, u32[]{:S(2)}) %collective-permute-start.3) | collective-permute-done | bytes 69664 | tf_op jit(solution)/shard_map/ppermute | solution.py:257
  12.5 2.8 %collective-permute-done.2 = f32[136,128]{1,0:T(8,128)S(1)} collective-permute-done((f32[136,128]{1,0:T(8,128)S(1)}, f32[136,128]{1,0:T(8,128)S(1)}, u32[]{:S(2)}, u32[]{:S(2)}) %collective-permute-start.2) | collective-permute-done | bytes 69664 | tf_op jit(solution)/shard_map/ppermute | solution.py:257
  15.3 0.0 collective-permute-done.1
  15.3 2.6 %collective-permute-start.6 = (f32[136,128]{1,0:T(8,128)S(1)}, f32[136,128]{1,0:T(8,128)S(1)}, u32[]{:S(2)}, u32[]{:S(2)}) collective-permute-start(f32[136,128]{1,0:T(8,128)S(1)} %add_add_fusion.1), channel_id=1, source_target_pairs={{0,20},{1,11},{2,22},{3,9},{4,16},{5,15},{6,18},{7,13},{8,28},{9,3... | collective-permute-start | bytes 208904 | tf_op jit(solution)/shard_map/ppermute | solution.py:257
  17.9 0.4 %collective-permute-start.5 = (f32[136,128]{1,0:T(8,128)S(1)}, f32[136,128]{1,0:T(8,128)S(1)}, u32[]{:S(2)}, u32[]{:S(2)}) collective-permute-start(f32[136,128]{1,0:T(8,128)S(1)} %add_add_fusion.1), channel_id=1, source_target_pairs={{0,4},{1,9},{2,6},{3,11},{4,0},{5,13},{6,2},{7,15},{8,12},{9,1},{1... | collective-permute-start | bytes 208904 | tf_op jit(solution)/shard_map/ppermute | solution.py:257
  18.3 0.5 %collective-permute-start.4 = (f32[136,128]{1,0:T(8,128)S(1)}, f32[136,128]{1,0:T(8,128)S(1)}, u32[]{:S(2)}, u32[]{:S(2)}) collective-permute-start(f32[136,128]{1,0:T(8,128)S(1)} %add_add_fusion.1), channel_id=1, source_target_pairs={{0,16},{1,3},{2,18},{3,1},{4,20},{5,7},{6,22},{7,5},{8,24},{9,11},... | collective-permute-start | bytes 208904 | tf_op jit(solution)/shard_map/ppermute | solution.py:257
  18.9 2.3 %collective-permute-done.6 = f32[136,128]{1,0:T(8,128)S(1)} collective-permute-done((f32[136,128]{1,0:T(8,128)S(1)}, f32[136,128]{1,0:T(8,128)S(1)}, u32[]{:S(2)}, u32[]{:S(2)}) %collective-permute-start.6) | collective-permute-done | bytes 69664 | tf_op jit(solution)/shard_map/ppermute | solution.py:257
  21.1 1.1 %collective-permute-done.5 = f32[136,128]{1,0:T(8,128)S(1)} collective-permute-done((f32[136,128]{1,0:T(8,128)S(1)}, f32[136,128]{1,0:T(8,128)S(1)}, u32[]{:S(2)}, u32[]{:S(2)}) %collective-permute-start.5) | collective-permute-done | bytes 69664 | tf_op jit(solution)/shard_map/ppermute | solution.py:257
  22.2 0.4 %collective-permute-done.4 = f32[136,128]{1,0:T(8,128)S(1)} collective-permute-done((f32[136,128]{1,0:T(8,128)S(1)}, f32[136,128]{1,0:T(8,128)S(1)}, u32[]{:S(2)}, u32[]{:S(2)}) %collective-permute-start.4) | collective-permute-done | bytes 69664 | tf_op jit(solution)/shard_map/ppermute | solution.py:257
  22.7 0.1 collective-permute-start.7
  22.8 1.2 %collective-permute-done.7 = f32[136,128]{1,0:T(8,128)S(1)} collective-permute-done((f32[136,128]{1,0:T(8,128)S(1)}, f32[136,128]{1,0:T(8,128)S(1)}, u32[]{:S(2)}, u32[]{:S(2)}) %collective-permute-start.7) | collective-permute-done | bytes 69664 | tf_op jit(solution)/shard_map/ppermute | solution.py:257
  24.0 6.5 %shard_map.59 = (f32[1024,256]{1,0:T(8,128)}, f32[256,256]{1,0:T(8,128)}, f32[1024,256]{1,0:T(8,128)}) custom-call(f32[272,128]{1,0:T(8,128)S(1)} %pad_maximum_fusion.packed_ref, bf16[1024,256]{1,0:T(8,128)(2,1)S(1)} %get-tuple-element.7.xh_ref, bf16[1024,256]{1,0:T(8,128)(2,1)S(1)} %get-tuple-element.8.xl_ref), custom_call_target="tpu_custom_call" | custom-call | tf_op jit(solution)/shard_map/pallas_call | solution.py:307
  (6 shorter events, 0.1 us)
Async XLA Ops:
  3.7 1.4 %collective-permute-start = (f32[136,128]{1,0:T(8,128)S(1)}, f32[136,128]{1,0:T(8,128)S(1)}, u32[]{:S(2)}, u32[]{:S(2)}) collective-permute-start(f32[136,128]{1,0:T(8,128)S(1)} %dynamic-slice_bitcast_fusion), channel_id=1, source_target_pairs={{0,1},{1,0},{2,3},{3,2},{4,5},{5,4},{6,7},{7,6},{8,9},{9,8},{10,11... | collective-permute-start | bytes 208904 | tf_op jit(solution)/shard_map/ppermute | solution.py:257
  5.1 7.3 %collective-permute-start.3 = (f32[136,128]{1,0:T(8,128)S(1)}, f32[136,128]{1,0:T(8,128)S(1)}, u32[]{:S(2)}, u32[]{:S(2)}) collective-permute-start(f32[136,128]{1,0:T(8,128)S(1)} %bitcast_add_fusion), channel_id=1, source_target_pairs={{0,10},{1,21},{2,8},{3,23},{4,14},{5,17},{6,12},{7,19},{8,2},{9,29... | collective-permute-start | bytes 208904 | tf_op jit(solution)/shard_map/ppermute | solution.py:257
  10.1 5.2 %collective-permute-start.2 = (f32[136,128]{1,0:T(8,128)S(1)}, f32[136,128]{1,0:T(8,128)S(1)}, u32[]{:S(2)}, u32[]{:S(2)}) collective-permute-start(f32[136,128]{1,0:T(8,128)S(1)} %bitcast_add_fusion), channel_id=1, source_target_pairs={{0,8},{1,5},{2,10},{3,7},{4,12},{5,1},{6,14},{7,3},{8,0},{9,13},{1... | collective-permute-start | bytes 208904 | tf_op jit(solution)/shard_map/ppermute | solution.py:257
  10.4 4.9 %collective-permute-start.1 = (f32[136,128]{1,0:T(8,128)S(1)}, f32[136,128]{1,0:T(8,128)S(1)}, u32[]{:S(2)}, u32[]{:S(2)}) collective-permute-start(f32[136,128]{1,0:T(8,128)S(1)} %bitcast_add_fusion), channel_id=1, source_target_pairs={{0,2},{1,17},{2,0},{3,19},{4,6},{5,21},{6,4},{7,23},{8,10},{9,25},... | collective-permute-start | bytes 208904 | tf_op jit(solution)/shard_map/ppermute | solution.py:257
  15.3 5.8 %collective-permute-start.6 = (f32[136,128]{1,0:T(8,128)S(1)}, f32[136,128]{1,0:T(8,128)S(1)}, u32[]{:S(2)}, u32[]{:S(2)}) collective-permute-start(f32[136,128]{1,0:T(8,128)S(1)} %add_add_fusion.1), channel_id=1, source_target_pairs={{0,20},{1,11},{2,22},{3,9},{4,16},{5,15},{6,18},{7,13},{8,28},{9,3... | collective-permute-start | bytes 208904 | tf_op jit(solution)/shard_map/ppermute | solution.py:257
  17.9 4.3 %collective-permute-start.5 = (f32[136,128]{1,0:T(8,128)S(1)}, f32[136,128]{1,0:T(8,128)S(1)}, u32[]{:S(2)}, u32[]{:S(2)}) collective-permute-start(f32[136,128]{1,0:T(8,128)S(1)} %add_add_fusion.1), channel_id=1, source_target_pairs={{0,4},{1,9},{2,6},{3,11},{4,0},{5,13},{6,2},{7,15},{8,12},{9,1},{1... | collective-permute-start | bytes 208904 | tf_op jit(solution)/shard_map/ppermute | solution.py:257
  18.3 4.3 %collective-permute-start.4 = (f32[136,128]{1,0:T(8,128)S(1)}, f32[136,128]{1,0:T(8,128)S(1)}, u32[]{:S(2)}, u32[]{:S(2)}) collective-permute-start(f32[136,128]{1,0:T(8,128)S(1)} %add_add_fusion.1), channel_id=1, source_target_pairs={{0,16},{1,3},{2,18},{3,1},{4,20},{5,7},{6,22},{7,5},{8,24},{9,11},... | collective-permute-start | bytes 208904 | tf_op jit(solution)/shard_map/ppermute | solution.py:257
  22.7 1.3 %collective-permute-start.7 = (f32[136,128]{1,0:T(8,128)S(1)}, f32[136,128]{1,0:T(8,128)S(1)}, u32[]{:S(2)}, u32[]{:S(2)}) collective-permute-start(f32[136,128]{1,0:T(8,128)S(1)} %add_add_fusion), channel_id=1, source_target_pairs={{0,1},{1,0},{2,3},{3,2},{4,5},{5,4},{6,7},{7,6},{8,9},{9,8},{10,11... | collective-permute-start | bytes 208904 | tf_op jit(solution)/shard_map/ppermute | solution.py:257

commit v7 on v6

--- a/solution.py
+++ b/solution.py
@@ -198,6 +198,8 @@
     left_lanes, right_lanes, all_lanes = pl.ds(0, HALF), pl.ds(HALF, HALF), pl.ds(0, 2 * HALF)
     factor(first, upper, inverse, update, lambda s: None)
     corner = full_dot(inverse[...], side)
+    missed = side - full_dot(upper[...].T, corner)
+    corner = corner + full_dot(inverse[...], missed)
     tri[:HALF, :HALF] = upper[...]
     tri[:HALF, HALF:] = corner
     tri[HALF:, :HALF] = jnp.zeros((HALF, HALF), jnp.float32)

time: 30.6 us -> 31 us (1.013)
  Pallas kernels: 8.83 us -> 9.22 us
    pallas_call x1, Pallas kernels: 6.46 us -> 6.85 us  [on_device(): pl.pallas_call(finish_kernel, in_specs=[vmem, vmem, vmem], out_specs=[hbm...]
where the time goes in v7:
time: 31 us; the launch traced here: 30.9 us
  waiting for transfers between devices  10.5 us (34%)
  starting transfers between devices  9.72 us (31%)
  Pallas kernels  9.22 us (30%)
  between operations  1.34 us (4%)
    ppermute x8, waiting for transfers between devices, flip(): return lax.ppermute(value, AXES, pairs)  10.5 us
    ppermute x8, starting transfers between devices, flip(): return lax.ppermute(value, AXES, pairs)  9.72 us
    pallas_call x1, Pallas kernels, on_device(): pl.pallas_call(finish_kernel, in_specs=[vmem, vmem, vmem], out_specs=[hbm...  6.85 us
    pallas_call x1, Pallas kernels, on_device(): pl.pallas_call(functools.partial(gram_kernel, total_rows=rows * devices),...  2.38 us
  transfers between devices with their start and end apart: 8, of which 7 were waited for; matrix products, arithmetic and copies ran while one was open for 0% of the time, Pallas kernels for 0%

profile of v7, /device:TPU:0, one launch (start us, length us, event | category | flops | bytes accessed | tf_op | source)
XLA Modules:
  0.0 30.9 jit_solution(5201220404300655048)
XLA Ops:
  1.3 2.4 %shard_map.58 = (f32[272,128]{1,0:T(8,128)S(1)}, bf16[1024,256]{1,0:T(8,128)(2,1)S(1)}, bf16[1024,256]{1,0:T(8,128)(2,1)S(1)}) custom-call(s32[1]{0:T(128)S(6)} %copy.6.live_ref, s32[1,256]{1,0:T(1,128)} %bitcast.8, f32[1024,256]{1,0:T(8,128)} %x_ref.1), custom_call_target="tpu_custom_call" | custom-call | tf_op jit(solution)/shard_map/pallas_call | solution.py:295
  3.7 0.5 %collective-permute-start = (f32[136,128]{1,0:T(8,128)S(1)}, f32[136,128]{1,0:T(8,128)S(1)}, u32[]{:S(2)}, u32[]{:S(2)}) collective-permute-start(f32[136,128]{1,0:T(8,128)S(1)} %dynamic-slice_bitcast_fusion), channel_id=1, source_target_pairs={{0,1},{1,0},{2,3},{3,2},{4,5},{5,4},{6,7},{7,6},{8,9},{9,8},{10,11... | collective-permute-start | bytes 208904 | tf_op jit(solution)/shard_map/ppermute | solution.py:259
  4.2 0.9 %collective-permute-done = f32[136,128]{1,0:T(8,128)S(1)} collective-permute-done((f32[136,128]{1,0:T(8,128)S(1)}, f32[136,128]{1,0:T(8,128)S(1)}, u32[]{:S(2)}, u32[]{:S(2)}) %collective-permute-start) | collective-permute-done | bytes 69664 | tf_op jit(solution)/shard_map/ppermute | solution.py:259
  5.1 4.9 %collective-permute-start.3 = (f32[136,128]{1,0:T(8,128)S(1)}, f32[136,128]{1,0:T(8,128)S(1)}, u32[]{:S(2)}, u32[]{:S(2)}) collective-permute-start(f32[136,128]{1,0:T(8,128)S(1)} %bitcast_add_fusion), channel_id=1, source_target_pairs={{0,10},{1,21},{2,8},{3,23},{4,14},{5,17},{6,12},{7,19},{8,2},{9,29... | collective-permute-start | bytes 208904 | tf_op jit(solution)/shard_map/ppermute | solution.py:259
  10.1 0.3 %collective-permute-start.2 = (f32[136,128]{1,0:T(8,128)S(1)}, f32[136,128]{1,0:T(8,128)S(1)}, u32[]{:S(2)}, u32[]{:S(2)}) collective-permute-start(f32[136,128]{1,0:T(8,128)S(1)} %bitcast_add_fusion), channel_id=1, source_target_pairs={{0,8},{1,5},{2,10},{3,7},{4,12},{5,1},{6,14},{7,3},{8,0},{9,13},{1... | collective-permute-start | bytes 208904 | tf_op jit(solution)/shard_map/ppermute | solution.py:259
  10.4 0.3 %collective-permute-start.1 = (f32[136,128]{1,0:T(8,128)S(1)}, f32[136,128]{1,0:T(8,128)S(1)}, u32[]{:S(2)}, u32[]{:S(2)}) collective-permute-start(f32[136,128]{1,0:T(8,128)S(1)} %bitcast_add_fusion), channel_id=1, source_target_pairs={{0,2},{1,17},{2,0},{3,19},{4,6},{5,21},{6,4},{7,23},{8,10},{9,25},... | collective-permute-start | bytes 208904 | tf_op jit(solution)/shard_map/ppermute | solution.py:259
  10.7 1.7 %collective-permute-done.3 = f32[136,128]{1,0:T(8,128)S(1)} collective-permute-done((f32[136,128]{1,0:T(8,128)S(1)}, f32[136,128]{1,0:T(8,128)S(1)}, u32[]{:S(2)}, u32[]{:S(2)}) %collective-permute-start.3) | collective-permute-done | bytes 69664 | tf_op jit(solution)/shard_map/ppermute | solution.py:259
  12.5 2.8 %collective-permute-done.2 = f32[136,128]{1,0:T(8,128)S(1)} collective-permute-done((f32[136,128]{1,0:T(8,128)S(1)}, f32[136,128]{1,0:T(8,128)S(1)}, u32[]{:S(2)}, u32[]{:S(2)}) %collective-permute-start.2) | collective-permute-done | bytes 69664 | tf_op jit(solution)/shard_map/ppermute | solution.py:259
  15.3 0.0 collective-permute-done.1
  15.3 2.6 %collective-permute-start.6 = (f32[136,128]{1,0:T(8,128)S(1)}, f32[136,128]{1,0:T(8,128)S(1)}, u32[]{:S(2)}, u32[]{:S(2)}) collective-permute-start(f32[136,128]{1,0:T(8,128)S(1)} %add_add_fusion.1), channel_id=1, source_target_pairs={{0,20},{1,11},{2,22},{3,9},{4,16},{5,15},{6,18},{7,13},{8,28},{9,3... | collective-permute-start | bytes 208904 | tf_op jit(solution)/shard_map/ppermute | solution.py:259
  17.9 0.4 %collective-permute-start.5 = (f32[136,128]{1,0:T(8,128)S(1)}, f32[136,128]{1,0:T(8,128)S(1)}, u32[]{:S(2)}, u32[]{:S(2)}) collective-permute-start(f32[136,128]{1,0:T(8,128)S(1)} %add_add_fusion.1), channel_id=1, source_target_pairs={{0,4},{1,9},{2,6},{3,11},{4,0},{5,13},{6,2},{7,15},{8,12},{9,1},{1... | collective-permute-start | bytes 208904 | tf_op jit(solution)/shard_map/ppermute | solution.py:259
  18.3 0.5 %collective-permute-start.4 = (f32[136,128]{1,0:T(8,128)S(1)}, f32[136,128]{1,0:T(8,128)S(1)}, u32[]{:S(2)}, u32[]{:S(2)}) collective-permute-start(f32[136,128]{1,0:T(8,128)S(1)} %add_add_fusion.1), channel_id=1, source_target_pairs={{0,16},{1,3},{2,18},{3,1},{4,20},{5,7},{6,22},{7,5},{8,24},{9,11},... | collective-permute-start | bytes 208904 | tf_op jit(solution)/shard_map/ppermute | solution.py:259
  18.9 2.3 %collective-permute-done.6 = f32[136,128]{1,0:T(8,128)S(1)} collective-permute-done((f32[136,128]{1,0:T(8,128)S(1)}, f32[136,128]{1,0:T(8,128)S(1)}, u32[]{:S(2)}, u32[]{:S(2)}) %collective-permute-start.6) | collective-permute-done | bytes 69664 | tf_op jit(solution)/shard_map/ppermute | solution.py:259
  21.1 1.1 %collective-permute-done.5 = f32[136,128]{1,0:T(8,128)S(1)} collective-permute-done((f32[136,128]{1,0:T(8,128)S(1)}, f32[136,128]{1,0:T(8,128)S(1)}, u32[]{:S(2)}, u32[]{:S(2)}) %collective-permute-start.5) | collective-permute-done | bytes 69664 | tf_op jit(solution)/shard_map/ppermute | solution.py:259
  22.2 0.4 %collective-permute-done.4 = f32[136,128]{1,0:T(8,128)S(1)} collective-permute-done((f32[136,128]{1,0:T(8,128)S(1)}, f32[136,128]{1,0:T(8,128)S(1)}, u32[]{:S(2)}, u32[]{:S(2)}) %collective-permute-start.4) | collective-permute-done | bytes 69664 | tf_op jit(solution)/shard_map/ppermute | solution.py:259
  22.7 0.1 collective-permute-start.7
  22.8 1.2 %collective-permute-done.7 = f32[136,128]{1,0:T(8,128)S(1)} collective-permute-done((f32[136,128]{1,0:T(8,128)S(1)}, f32[136,128]{1,0:T(8,128)S(1)}, u32[]{:S(2)}, u32[]{:S(2)}) %collective-permute-start.7) | collective-permute-done | bytes 69664 | tf_op jit(solution)/shard_map/ppermute | solution.py:259
  24.0 6.8 %shard_map.59 = (f32[1024,256]{1,0:T(8,128)}, f32[256,256]{1,0:T(8,128)}, f32[1024,256]{1,0:T(8,128)}) custom-call(f32[272,128]{1,0:T(8,128)S(1)} %pad_maximum_fusion.packed_ref, bf16[1024,256]{1,0:T(8,128)(2,1)S(1)} %get-tuple-element.7.xh_ref, bf16[1024,256]{1,0:T(8,128)(2,1)S(1)} %get-tuple-element.8.xl_ref), custom_call_target="tpu_custom_call" | custom-call | tf_op jit(solution)/shard_map/pallas_call | solution.py:309
  (6 shorter events, 0.1 us)
Async XLA Ops:
  3.7 1.4 %collective-permute-start = (f32[136,128]{1,0:T(8,128)S(1)}, f32[136,128]{1,0:T(8,128)S(1)}, u32[]{:S(2)}, u32[]{:S(2)}) collective-permute-start(f32[136,128]{1,0:T(8,128)S(1)} %dynamic-slice_bitcast_fusion), channel_id=1, source_target_pairs={{0,1},{1,0},{2,3},{3,2},{4,5},{5,4},{6,7},{7,6},{8,9},{9,8},{10,11... | collective-permute-start | bytes 208904 | tf_op jit(solution)/shard_map/ppermute | solution.py:259
  5.1 7.3 %collective-permute-start.3 = (f32[136,128]{1,0:T(8,128)S(1)}, f32[136,128]{1,0:T(8,128)S(1)}, u32[]{:S(2)}, u32[]{:S(2)}) collective-permute-start(f32[136,128]{1,0:T(8,128)S(1)} %bitcast_add_fusion), channel_id=1, source_target_pairs={{0,10},{1,21},{2,8},{3,23},{4,14},{5,17},{6,12},{7,19},{8,2},{9,29... | collective-permute-start | bytes 208904 | tf_op jit(solution)/shard_map/ppermute | solution.py:259
  10.1 5.2 %collective-permute-start.2 = (f32[136,128]{1,0:T(8,128)S(1)}, f32[136,128]{1,0:T(8,128)S(1)}, u32[]{:S(2)}, u32[]{:S(2)}) collective-permute-start(f32[136,128]{1,0:T(8,128)S(1)} %bitcast_add_fusion), channel_id=1, source_target_pairs={{0,8},{1,5},{2,10},{3,7},{4,12},{5,1},{6,14},{7,3},{8,0},{9,13},{1... | collective-permute-start | bytes 208904 | tf_op jit(solution)/shard_map/ppermute | solution.py:259
  10.4 4.9 %collective-permute-start.1 = (f32[136,128]{1,0:T(8,128)S(1)}, f32[136,128]{1,0:T(8,128)S(1)}, u32[]{:S(2)}, u32[]{:S(2)}) collective-permute-start(f32[136,128]{1,0:T(8,128)S(1)} %bitcast_add_fusion), channel_id=1, source_target_pairs={{0,2},{1,17},{2,0},{3,19},{4,6},{5,21},{6,4},{7,23},{8,10},{9,25},... | collective-permute-start | bytes 208904 | tf_op jit(solution)/shard_map/ppermute | solution.py:259
  15.3 5.8 %collective-permute-start.6 = (f32[136,128]{1,0:T(8,128)S(1)}, f32[136,128]{1,0:T(8,128)S(1)}, u32[]{:S(2)}, u32[]{:S(2)}) collective-permute-start(f32[136,128]{1,0:T(8,128)S(1)} %add_add_fusion.1), channel_id=1, source_target_pairs={{0,20},{1,11},{2,22},{3,9},{4,16},{5,15},{6,18},{7,13},{8,28},{9,3... | collective-permute-start | bytes 208904 | tf_op jit(solution)/shard_map/ppermute | solution.py:259
  17.9 4.3 %collective-permute-start.5 = (f32[136,128]{1,0:T(8,128)S(1)}, f32[136,128]{1,0:T(8,128)S(1)}, u32[]{:S(2)}, u32[]{:S(2)}) collective-permute-start(f32[136,128]{1,0:T(8,128)S(1)} %add_add_fusion.1), channel_id=1, source_target_pairs={{0,4},{1,9},{2,6},{3,11},{4,0},{5,13},{6,2},{7,15},{8,12},{9,1},{1... | collective-permute-start | bytes 208904 | tf_op jit(solution)/shard_map/ppermute | solution.py:259
  18.3 4.3 %collective-permute-start.4 = (f32[136,128]{1,0:T(8,128)S(1)}, f32[136,128]{1,0:T(8,128)S(1)}, u32[]{:S(2)}, u32[]{:S(2)}) collective-permute-start(f32[136,128]{1,0:T(8,128)S(1)} %add_add_fusion.1), channel_id=1, source_target_pairs={{0,16},{1,3},{2,18},{3,1},{4,20},{5,7},{6,22},{7,5},{8,24},{9,11},... | collective-permute-start | bytes 208904 | tf_op jit(solution)/shard_map/ppermute | solution.py:259
  22.7 1.3 %collective-permute-start.7 = (f32[136,128]{1,0:T(8,128)S(1)}, f32[136,128]{1,0:T(8,128)S(1)}, u32[]{:S(2)}, u32[]{:S(2)}) collective-permute-start(f32[136,128]{1,0:T(8,128)S(1)} %add_add_fusion), channel_id=1, source_target_pairs={{0,1},{1,0},{2,3},{3,2},{4,5},{5,4},{6,7},{7,6},{8,9},{9,8},{10,11... | collective-permute-start | bytes 208904 | tf_op jit(solution)/shard_map/ppermute | solution.py:259

commit v8 on v7

--- a/solution.py
+++ b/solution.py
@@ -195,11 +195,19 @@
         )
         copies[-1].start()
 
+    def fold(value):
+        return value[:, :HALF] + value[:, HALF:]
+
     left_lanes, right_lanes, all_lanes = pl.ds(0, HALF), pl.ds(HALF, HALF), pl.ds(0, 2 * HALF)
     factor(first, upper, inverse, update, lambda s: None)
     corner = full_dot(inverse[...], side)
     missed = side - full_dot(upper[...].T, corner)
-    corner = corner + full_dot(inverse[...], missed)
+    ih, im, _ = thirds(inverse[...])
+    mh, mm, _ = thirds(missed)
+    pair = jnp.concatenate([mh, mm], 1)
+    corner = corner + fold(
+        dot(jnp.concatenate([ih, im], 1), jnp.concatenate([pair, pair], 0))
+    )
     tri[:HALF, :HALF] = upper[...]
     tri[:HALF, HALF:] = corner
     tri[HALF:, :HALF] = jnp.zeros((HALF, HALF), jnp.float32)
@@ -210,9 +218,6 @@
     def inverse_weights():
         h, l = halves(inverse[...])
         return jnp.concatenate([jnp.concatenate([h, h], 1), jnp.concatenate([l, none], 1)], 0)
-
-    def fold(value):
-        return value[:, :HALF] + value[:, HALF:]
 
     to_left = inverse_weights()
     ch, cl = halves(corner)

time: 31 us -> 31 us (level)
  no operation moved by 1% of the time
where the time goes in v8:
time: 31 us; the launch traced here: 30.9 us
  waiting for transfers between devices  10.5 us (34%)
  starting transfers between devices  9.72 us (31%)
  Pallas kernels  9.21 us (30%)
  between operations  1.34 us (4%)
    ppermute x8, waiting for transfers between devices, flip(): return lax.ppermute(value, AXES, pairs)  10.5 us
    ppermute x8, starting transfers between devices, flip(): return lax.ppermute(value, AXES, pairs)  9.72 us
    pallas_call x1, Pallas kernels, on_device(): pl.pallas_call(finish_kernel, in_specs=[vmem, vmem, vmem], out_specs=[hbm...  6.83 us
    pallas_call x1, Pallas kernels, on_device(): pl.pallas_call(functools.partial(gram_kernel, total_rows=rows * devices),...  2.38 us
  transfers between devices with their start and end apart: 8, of which 7 were waited for; matrix products, arithmetic and copies ran while one was open for 0% of the time, Pallas kernels for 0%

profile of v8, /device:TPU:0, one launch (start us, length us, event | category | flops | bytes accessed | tf_op | source)
XLA Modules:
  0.0 30.9 jit_solution(13173309640529249148)
XLA Ops:
  1.3 2.4 %shard_map.58 = (f32[272,128]{1,0:T(8,128)S(1)}, bf16[1024,256]{1,0:T(8,128)(2,1)S(1)}, bf16[1024,256]{1,0:T(8,128)(2,1)S(1)}) custom-call(s32[1]{0:T(128)S(6)} %copy.6.live_ref, s32[1,256]{1,0:T(1,128)} %bitcast.8, f32[1024,256]{1,0:T(8,128)} %x_ref.1), custom_call_target="tpu_custom_call" | custom-call | tf_op jit(solution)/shard_map/pallas_call | solution.py:300
  3.7 0.5 %collective-permute-start = (f32[136,128]{1,0:T(8,128)S(1)}, f32[136,128]{1,0:T(8,128)S(1)}, u32[]{:S(2)}, u32[]{:S(2)}) collective-permute-start(f32[136,128]{1,0:T(8,128)S(1)} %dynamic-slice_bitcast_fusion), channel_id=1, source_target_pairs={{0,1},{1,0},{2,3},{3,2},{4,5},{5,4},{6,7},{7,6},{8,9},{9,8},{10,11... | collective-permute-start | bytes 208904 | tf_op jit(solution)/shard_map/ppermute | solution.py:264
  4.2 0.9 %collective-permute-done = f32[136,128]{1,0:T(8,128)S(1)} collective-permute-done((f32[136,128]{1,0:T(8,128)S(1)}, f32[136,128]{1,0:T(8,128)S(1)}, u32[]{:S(2)}, u32[]{:S(2)}) %collective-permute-start) | collective-permute-done | bytes 69664 | tf_op jit(solution)/shard_map/ppermute | solution.py:264
  5.1 4.9 %collective-permute-start.3 = (f32[136,128]{1,0:T(8,128)S(1)}, f32[136,128]{1,0:T(8,128)S(1)}, u32[]{:S(2)}, u32[]{:S(2)}) collective-permute-start(f32[136,128]{1,0:T(8,128)S(1)} %bitcast_add_fusion), channel_id=1, source_target_pairs={{0,10},{1,21},{2,8},{3,23},{4,14},{5,17},{6,12},{7,19},{8,2},{9,29... | collective-permute-start | bytes 208904 | tf_op jit(solution)/shard_map/ppermute | solution.py:264
  10.1 0.3 %collective-permute-start.2 = (f32[136,128]{1,0:T(8,128)S(1)}, f32[136,128]{1,0:T(8,128)S(1)}, u32[]{:S(2)}, u32[]{:S(2)}) collective-permute-start(f32[136,128]{1,0:T(8,128)S(1)} %bitcast_add_fusion), channel_id=1, source_target_pairs={{0,8},{1,5},{2,10},{3,7},{4,12},{5,1},{6,14},{7,3},{8,0},{9,13},{1... | collective-permute-start | bytes 208904 | tf_op jit(solution)/shard_map/ppermute | solution.py:264
  10.4 0.3 %collective-permute-start.1 = (f32[136,128]{1,0:T(8,128)S(1)}, f32[136,128]{1,0:T(8,128)S(1)}, u32[]{:S(2)}, u32[]{:S(2)}) collective-permute-start(f32[136,128]{1,0:T(8,128)S(1)} %bitcast_add_fusion), channel_id=1, source_target_pairs={{0,2},{1,17},{2,0},{3,19},{4,6},{5,21},{6,4},{7,23},{8,10},{9,25},... | collective-permute-start | bytes 208904 | tf_op jit(solution)/shard_map/ppermute | solution.py:264
  10.7 1.7 %collective-permute-done.3 = f32[136,128]{1,0:T(8,128)S(1)} collective-permute-done((f32[136,128]{1,0:T(8,128)S(1)}, f32[136,128]{1,0:T(8,128)S(1)}, u32[]{:S(2)}, u32[]{:S(2)}) %collective-permute-start.3) | collective-permute-done | bytes 69664 | tf_op jit(solution)/shard_map/ppermute | solution.py:264
  12.5 2.8 %collective-permute-done.2 = f32[136,128]{1,0:T(8,128)S(1)} collective-permute-done((f32[136,128]{1,0:T(8,128)S(1)}, f32[136,128]{1,0:T(8,128)S(1)}, u32[]{:S(2)}, u32[]{:S(2)}) %collective-permute-start.2) | collective-permute-done | bytes 69664 | tf_op jit(solution)/shard_map/ppermute | solution.py:264
  15.3 0.0 collective-permute-done.1
  15.3 2.6 %collective-permute-start.6 = (f32[136,128]{1,0:T(8,128)S(1)}, f32[136,128]{1,0:T(8,128)S(1)}, u32[]{:S(2)}, u32[]{:S(2)}) collective-permute-start(f32[136,128]{1,0:T(8,128)S(1)} %add_add_fusion.1), channel_id=1, source_target_pairs={{0,20},{1,11},{2,22},{3,9},{4,16},{5,15},{6,18},{7,13},{8,28},{9,3... | collective-permute-start | bytes 208904 | tf_op jit(solution)/shard_map/ppermute | solution.py:264
  17.9 0.4 %collective-permute-start.5 = (f32[136,128]{1,0:T(8,128)S(1)}, f32[136,128]{1,0:T(8,128)S(1)}, u32[]{:S(2)}, u32[]{:S(2)}) collective-permute-start(f32[136,128]{1,0:T(8,128)S(1)} %add_add_fusion.1), channel_id=1, source_target_pairs={{0,4},{1,9},{2,6},{3,11},{4,0},{5,13},{6,2},{7,15},{8,12},{9,1},{1... | collective-permute-start | bytes 208904 | tf_op jit(solution)/shard_map/ppermute | solution.py:264
  18.3 0.5 %collective-permute-start.4 = (f32[136,128]{1,0:T(8,128)S(1)}, f32[136,128]{1,0:T(8,128)S(1)}, u32[]{:S(2)}, u32[]{:S(2)}) collective-permute-start(f32[136,128]{1,0:T(8,128)S(1)} %add_add_fusion.1), channel_id=1, source_target_pairs={{0,16},{1,3},{2,18},{3,1},{4,20},{5,7},{6,22},{7,5},{8,24},{9,11},... | collective-permute-start | bytes 208904 | tf_op jit(solution)/shard_map/ppermute | solution.py:264
  18.9 2.3 %collective-permute-done.6 = f32[136,128]{1,0:T(8,128)S(1)} collective-permute-done((f32[136,128]{1,0:T(8,128)S(1)}, f32[136,128]{1,0:T(8,128)S(1)}, u32[]{:S(2)}, u32[]{:S(2)}) %collective-permute-start.6) | collective-permute-done | bytes 69664 | tf_op jit(solution)/shard_map/ppermute | solution.py:264
  21.1 1.1 %collective-permute-done.5 = f32[136,128]{1,0:T(8,128)S(1)} collective-permute-done((f32[136,128]{1,0:T(8,128)S(1)}, f32[136,128]{1,0:T(8,128)S(1)}, u32[]{:S(2)}, u32[]{:S(2)}) %collective-permute-start.5) | collective-permute-done | bytes 69664 | tf_op jit(solution)/shard_map/ppermute | solution.py:264
  22.2 0.4 %collective-permute-done.4 = f32[136,128]{1,0:T(8,128)S(1)} collective-permute-done((f32[136,128]{1,0:T(8,128)S(1)}, f32[136,128]{1,0:T(8,128)S(1)}, u32[]{:S(2)}, u32[]{:S(2)}) %collective-permute-start.4) | collective-permute-done | bytes 69664 | tf_op jit(solution)/shard_map/ppermute | solution.py:264
  22.7 0.1 collective-permute-start.7
  22.8 1.2 %collective-permute-done.7 = f32[136,128]{1,0:T(8,128)S(1)} collective-permute-done((f32[136,128]{1,0:T(8,128)S(1)}, f32[136,128]{1,0:T(8,128)S(1)}, u32[]{:S(2)}, u32[]{:S(2)}) %collective-permute-start.7) | collective-permute-done | bytes 69664 | tf_op jit(solution)/shard_map/ppermute | solution.py:264
  24.0 6.8 %shard_map.59 = (f32[1024,256]{1,0:T(8,128)}, f32[256,256]{1,0:T(8,128)}, f32[1024,256]{1,0:T(8,128)}) custom-call(f32[272,128]{1,0:T(8,128)S(1)} %pad_maximum_fusion.packed_ref, bf16[1024,256]{1,0:T(8,128)(2,1)S(1)} %get-tuple-element.7.xh_ref, bf16[1024,256]{1,0:T(8,128)(2,1)S(1)} %get-tuple-element.8.xl_ref), custom_call_target="tpu_custom_call" | custom-call | tf_op jit(solution)/shard_map/pallas_call | solution.py:314
  (6 shorter events, 0.1 us)
Async XLA Ops:
  3.7 1.4 %collective-permute-start = (f32[136,128]{1,0:T(8,128)S(1)}, f32[136,128]{1,0:T(8,128)S(1)}, u32[]{:S(2)}, u32[]{:S(2)}) collective-permute-start(f32[136,128]{1,0:T(8,128)S(1)} %dynamic-slice_bitcast_fusion), channel_id=1, source_target_pairs={{0,1},{1,0},{2,3},{3,2},{4,5},{5,4},{6,7},{7,6},{8,9},{9,8},{10,11... | collective-permute-start | bytes 208904 | tf_op jit(solution)/shard_map/ppermute | solution.py:264
  5.1 7.3 %collective-permute-start.3 = (f32[136,128]{1,0:T(8,128)S(1)}, f32[136,128]{1,0:T(8,128)S(1)}, u32[]{:S(2)}, u32[]{:S(2)}) collective-permute-start(f32[136,128]{1,0:T(8,128)S(1)} %bitcast_add_fusion), channel_id=1, source_target_pairs={{0,10},{1,21},{2,8},{3,23},{4,14},{5,17},{6,12},{7,19},{8,2},{9,29... | collective-permute-start | bytes 208904 | tf_op jit(solution)/shard_map/ppermute | solution.py:264
  10.1 5.2 %collective-permute-start.2 = (f32[136,128]{1,0:T(8,128)S(1)}, f32[136,128]{1,0:T(8,128)S(1)}, u32[]{:S(2)}, u32[]{:S(2)}) collective-permute-start(f32[136,128]{1,0:T(8,128)S(1)} %bitcast_add_fusion), channel_id=1, source_target_pairs={{0,8},{1,5},{2,10},{3,7},{4,12},{5,1},{6,14},{7,3},{8,0},{9,13},{1... | collective-permute-start | bytes 208904 | tf_op jit(solution)/shard_map/ppermute | solution.py:264
  10.4 4.9 %collective-permute-start.1 = (f32[136,128]{1,0:T(8,128)S(1)}, f32[136,128]{1,0:T(8,128)S(1)}, u32[]{:S(2)}, u32[]{:S(2)}) collective-permute-start(f32[136,128]{1,0:T(8,128)S(1)} %bitcast_add_fusion), channel_id=1, source_target_pairs={{0,2},{1,17},{2,0},{3,19},{4,6},{5,21},{6,4},{7,23},{8,10},{9,25},... | collective-permute-start | bytes 208904 | tf_op jit(solution)/shard_map/ppermute | solution.py:264
  15.3 5.8 %collective-permute-start.6 = (f32[136,128]{1,0:T(8,128)S(1)}, f32[136,128]{1,0:T(8,128)S(1)}, u32[]{:S(2)}, u32[]{:S(2)}) collective-permute-start(f32[136,128]{1,0:T(8,128)S(1)} %add_add_fusion.1), channel_id=1, source_target_pairs={{0,20},{1,11},{2,22},{3,9},{4,16},{5,15},{6,18},{7,13},{8,28},{9,3... | collective-permute-start | bytes 208904 | tf_op jit(solution)/shard_map/ppermute | solution.py:264
  17.9 4.3 %collective-permute-start.5 = (f32[136,128]{1,0:T(8,128)S(1)}, f32[136,128]{1,0:T(8,128)S(1)}, u32[]{:S(2)}, u32[]{:S(2)}) collective-permute-start(f32[136,128]{1,0:T(8,128)S(1)} %add_add_fusion.1), channel_id=1, source_target_pairs={{0,4},{1,9},{2,6},{3,11},{4,0},{5,13},{6,2},{7,15},{8,12},{9,1},{1... | collective-permute-start | bytes 208904 | tf_op jit(solution)/shard_map/ppermute | solution.py:264
  18.3 4.3 %collective-permute-start.4 = (f32[136,128]{1,0:T(8,128)S(1)}, f32[136,128]{1,0:T(8,128)S(1)}, u32[]{:S(2)}, u32[]{:S(2)}) collective-permute-start(f32[136,128]{1,0:T(8,128)S(1)} %add_add_fusion.1), channel_id=1, source_target_pairs={{0,16},{1,3},{2,18},{3,1},{4,20},{5,7},{6,22},{7,5},{8,24},{9,11},... | collective-permute-start | bytes 208904 | tf_op jit(solution)/shard_map/ppermute | solution.py:264
  22.7 1.3 %collective-permute-start.7 = (f32[136,128]{1,0:T(8,128)S(1)}, f32[136,128]{1,0:T(8,128)S(1)}, u32[]{:S(2)}, u32[]{:S(2)}) collective-permute-start(f32[136,128]{1,0:T(8,128)S(1)} %add_add_fusion), channel_id=1, source_target_pairs={{0,1},{1,0},{2,3},{3,2},{4,5},{5,4},{6,7},{7,6},{8,9},{9,8},{10,11... | collective-permute-start | bytes 208904 | tf_op jit(solution)/shard_map/ppermute | solution.py:264
